TPU v7x, 1024 devices: a whole 4x4x32 slice. The times are simulated.
1024 devices in a mesh: ep: 16 (over x, y_lo, core), dp: 64 (over y_hi, z).
Axes of the slice: x: 4, y: 4 (y_hi: 2, y_lo: 2; y = y_hi * 2 + y_lo), z: 32, core: 2. Of those that a mesh axis runs over, the one named last changes fastest.
Arguments:
- tokens: bfloat16 [2048, 3584], P('dp'), may hold values from -6 to 6
- gate_scores: float32 [2048, 8], P('dp'), may hold values from 0.05 to 1
- routes: int32 [2048, 8], P('dp'), may hold values from 0 to 127, all different within a row; in each aligned block of 32 rows (0 to 31, 32 to 63, ...) at most 4 rows name the same one
- balanced: int32 [64, 16], P(None, 'ep'), may hold values from 0 to 1, as said below
- gate_up: bfloat16 [64, 16, 3584, 256], P('dp', 'ep'), may hold values from -0.09375 to 0.09375
- down_proj: bfloat16 [64, 16, 128, 3584], P('dp', 'ep'), may hold values from -0.1875 to 0.1875
Outputs:
- mixed: float32 [2048, 3584], P('dp', 'ep')
Inputs may be any that keep to these rules, and one draw needn't show every extreme that they name: `routes`: among the tokens of one dp index no expert is named more than 4 times, a bound that some block reaches. balanced[d, i] equals balanced[d + 32, i] for d < 32.
All inputs are finite; a program needn't handle non-finite values.
Results may differ from a plain program's by a relative error of at most 0.007.
Values may be sent and summed in bfloat16 or wider, within the bound.
No kernel may reach another device: no remote copies, remote signals or barrier semaphores. Data moves between devices by JAX's collectives and lax.ppermute only.
A program may use at most 64 MiB of HBM per device.

v0:
```python
import jax
import jax.numpy as jnp
from jax import lax
from jax.sharding import PartitionSpec as P

ROUTE_SCALE = 2.5


def swapped(value, axis, bit):
    mask = 2**bit
    pairs = [(source, source ^ mask) for source in range(lax.axis_size(axis))]
    return lax.ppermute(value, axis, pairs)


def tile_mlp(inputs, weight_up, weight_down):
    width = inputs.shape[-1]
    hidden_width = weight_down.shape[0]
    flat = inputs.reshape(-1, width)
    projected = jnp.dot(flat, weight_up, preferred_element_type=jnp.float32)
    hidden = (jax.nn.silu(projected[:, :hidden_width]) * projected[:, hidden_width:]).astype(
        jnp.bfloat16
    )
    result = jnp.dot(hidden, weight_down, preferred_element_type=jnp.float32).astype(jnp.bfloat16)
    return result.reshape(inputs.shape)


def per_device(tokens, gate_scores, routes, balanced, gate_up, down_proj):
    dp_count = lax.axis_size("dp")
    ep_count = lax.axis_size("ep")
    split_count = min(8, ep_count)
    per_line = ep_count // split_count
    expert_count = dp_count * per_line
    tok_rows, top_count = routes.shape
    capacity = min(tok_rows, max(2, 2 * tok_rows * top_count // expert_count))
    swap_bit = dp_count.bit_length() - 2
    dp_rank = lax.axis_index("dp")
    ep_rank = lax.axis_index("ep")
    flags = balanced[:, 0] == 1
    own_flag = flags[dp_rank]
    own_up = gate_up[0, 0]
    own_down = down_proj[0, 0]
    targets = jnp.arange(dp_count, dtype=jnp.int32)
    expert_at = targets * per_line + ep_rank // split_count
    flat_routes = routes.reshape(-1)
    matches = (flat_routes[:, None] == expert_at[None, :]).astype(jnp.int32)
    ranks = jnp.cumsum(matches, axis=0) - matches
    slot_ids = jnp.arange(capacity, dtype=jnp.int32)
    hits = matches[:, :, None] * (ranks[:, :, None] == slot_ids[None, None, :]).astype(jnp.int32)
    hits = hits.reshape(tok_rows, top_count, dp_count, capacity).astype(jnp.float32)
    selector = jnp.sum(hits, axis=1)
    scaled = gate_scores / jnp.sum(gate_scores, axis=1, keepdims=True) * ROUTE_SCALE
    slot_weight = jnp.einsum("tk,tkdc->dc", scaled, hits, precision=lax.Precision.HIGHEST)
    outgoing = jnp.einsum(
        "tdc,tf->dcf", selector.astype(jnp.bfloat16), tokens, preferred_element_type=jnp.float32
    ).astype(jnp.bfloat16)
    other_up, other_down = swapped((own_up, own_down), "dp", swap_bit)
    use_up = jnp.where(own_flag, other_up, own_up)
    use_down = jnp.where(own_flag, other_down, own_down)
    partial_value = tile_mlp(
        lax.all_to_all(outgoing, "dp", split_axis=0, concat_axis=0, tiled=True), use_up, use_down
    )
    returned = lax.all_to_all(partial_value, "dp", split_axis=0, concat_axis=0, tiled=True)
    weighted = returned.astype(jnp.float32) * slot_weight[:, :, None]
    contrib = jnp.einsum("tdc,dcf->tf", selector, weighted, precision=lax.Precision.HIGHEST)
    mixed = lax.psum_scatter(contrib, "ep", scatter_dimension=1, tiled=True)
    return mixed


def solution(mesh):
    placed = (
        P("dp", None),
        P("dp", None),
        P("dp", None),
        P(None, "ep"),
        P("dp", "ep", None, None),
        P("dp", "ep", None, None),
    )
    return jax.shard_map(
        per_device, mesh=mesh, in_specs=placed, out_specs=P("dp", "ep"), check_vma=False
    )
```

profile of v0, /device:TPU:6, one launch (start us, length us, event | category | flops | bytes accessed | tf_op | source)
XLA Modules:
  0.0 491.6 jit_solution(12036508490168182209)
XLA Ops:
  6.5 0.0 copy-start
  6.5 0.8 copy.24
  7.3 0.1 eq.62
  7.4 0.1 eq.58
  7.5 0.1 compare_convert_fusion
  7.7 0.1 compare_convert_fusion.1
  7.7 0.6 reduce-window.6
  8.3 0.2 slice_reduce_fusion
  8.6 0.1 fusion.11
  8.7 0.1 copy.27
  8.8 0.2 fusion.14
  9.0 0.0 copy-done
  9.0 0.7 convolution_convert_fusion.1
  9.7 2.6 copy.30
  12.3 0.0 copy-start.1
  12.3 0.0 copy-start.3
  12.3 32.1 %all-to-all-start = ((bf16[64,4,3584]{2,1,0:T(4,128)(2,1)}), bf16[64,4,3584]{2,1,0:T(4,128)(2,1)S(1)}, u32[]{:S(2)}, u32[]{:S(2)}) async-start(bf16[64,4,3584]{2,1,0:T(4,128)(2,1)} %copy.30), calls=%async_computation | async-start | bytes 3670016 | tf_op jit(solution)/shard_map/all_to_all | solution.py:60
  44.4 5.1 %collective-permute-start = (bf16[3584,256]{1,0:T(8,128)(2,1)}, bf16[3584,256]{1,0:T(8,128)(2,1)}, u32[]{:S(2)}, u32[]{:S(2)}) collective-permute-start(bf16[3584,256]{1,0:T(8,128)(2,1)} %bitcast.44), channel_id=1, source_target_pairs={{0,32},{1,33},{2,34},{3,35},{4,36},{5,37},{6,38},{7,39},{8,40},{9,... | collective-permute-start | bytes 5505032 | tf_op jit(solution)/shard_map/ppermute | solution.py:12
  49.5 0.0 copy-done.1
  49.6 2.3 collective-permute-start.1
  51.8 0.0 copy-done.3
  51.8 0.6 constant_dynamic-slice_fusion
  52.4 159.1 %all-to-all-done = bf16[64,4,3584]{2,1,0:T(4,128)(2,1)S(1)} async-done(((bf16[64,4,3584]{2,1,0:T(4,128)(2,1)}), bf16[64,4,3584]{2,1,0:T(4,128)(2,1)S(1)}, u32[]{:S(2)}, u32[]{:S(2)}) %all-to-all-start) | async-done | bytes 1835040 | tf_op jit(solution)/shard_map/all_to_all | solution.py:60
  211.6 1.4 reshape.72
  213.0 0.0 collective-permute-done
  213.0 3.9 fusion.1
  216.9 0.0 collective-permute-done.1
  216.9 2.5 convolution_convert_fusion
  219.4 1.5 reshape.73
  220.9 0.0 copy-start.2
  220.9 15.7 %all-to-all-start.1 = ((bf16[64,4,3584]{2,1,0:T(4,128)(2,1)}), bf16[64,4,3584]{2,1,0:T(4,128)(2,1)S(1)}, u32[]{:S(2)}, u32[]{:S(2)}) async-start(bf16[64,4,3584]{2,1,0:T(4,128)(2,1)} %reshape.73), calls=%async_computation.1 | async-start | bytes 3670016 | tf_op jit(solution)/shard_map/all_to_all | solution.py:62
  236.6 0.2 reduce-scatter.4.cloned.1.call-start
  236.8 0.0 copy-done.2
  236.9 0.1 select_convert_fusion
  236.9 0.6 fusion.6
  237.6 0.1 copy.35
  237.7 166.1 %all-to-all-done.1 = bf16[64,4,3584]{2,1,0:T(4,128)(2,1)S(1)} async-done(((bf16[64,4,3584]{2,1,0:T(4,128)(2,1)}), bf16[64,4,3584]{2,1,0:T(4,128)(2,1)S(1)}, u32[]{:S(2)}, u32[]{:S(2)}) %all-to-all-start.1) | async-done | bytes 1835040 | tf_op jit(solution)/shard_map/all_to_all | solution.py:62
  403.7 0.8 convert_multiply_fusion
  404.5 12.9 %convolution_bitcast_fusion = f32[3584,32]{1,0:T(8,128)} fusion(f32[64,4,3584]{2,1,0:T(4,128)S(1)} %convert_multiply_fusion, f32[32,64,4]{1,2,0:T(4,128)S(1)} %fusion.14), kind=kOutput, calls=%fused_computation.2 | convolution fusion | flops 352321536 | bytes 4161536 | tf_op jit(solution)/shard_map/tdc,dcf->tf/dot_general | solution.py:64
  417.5 0.0 reduce-scatter.4.cloned.1.call-update
  417.5 65.7 %reduce-scatter.4.cloned.1.call-done = f32[224,32]{1,0:T(8,128)} async-done(((f32[3584,32]{1,0:T(8,128)}), f32[224,32]{1,0:T(8,128)}) %reduce-scatter.4.cloned.1.call-update) | async-done | bytes 28688
  483.2 1.6 copy.37
  (7 shorter events, 0.1 us)
Async XLA Ops:
  6.5 2.5 copy-start
  12.3 37.2 %copy-start.1 = (bf16[1,1,128,3584]{3,2,1,0:T(8,128)(2,1)S(1)}, bf16[1,1,128,3584]{3,2,1,0:T(8,128)(2,1)}, u32[]{:S(2)}) copy-start(bf16[1,1,128,3584]{3,2,1,0:T(8,128)(2,1)} %param.11) | copy-start | bytes 2752516
  12.3 39.5 %copy-start.3 = (s32[64,1]{0,1:T(1,128)S(1)}, s32[64,1]{0,1:T(1,128)}, u32[]{:S(2)}) copy-start(s32[64,1]{0,1:T(1,128)} %param.9) | copy-start | bytes 772
  12.3 199.2 %all-to-all-start = ((bf16[64,4,3584]{2,1,0:T(4,128)(2,1)}), bf16[64,4,3584]{2,1,0:T(4,128)(2,1)S(1)}, u32[]{:S(2)}, u32[]{:S(2)}) async-start(bf16[64,4,3584]{2,1,0:T(4,128)(2,1)} %copy.30), calls=%async_computation | async-start | bytes 3670016 | tf_op jit(solution)/shard_map/all_to_all | solution.py:60
  44.4 168.6 %collective-permute-start = (bf16[3584,256]{1,0:T(8,128)(2,1)}, bf16[3584,256]{1,0:T(8,128)(2,1)}, u32[]{:S(2)}, u32[]{:S(2)}) collective-permute-start(bf16[3584,256]{1,0:T(8,128)(2,1)} %bitcast.44), channel_id=1, source_target_pairs={{0,32},{1,33},{2,34},{3,35},{4,36},{5,37},{6,38},{7,39},{8,40},{9,... | collective-permute-start | bytes 5505032 | tf_op jit(solution)/shard_map/ppermute | solution.py:12
  49.6 167.4 %collective-permute-start.1 = (bf16[128,3584]{1,0:T(8,128)(2,1)S(1)}, bf16[128,3584]{1,0:T(8,128)(2,1)}, u32[]{:S(2)}, u32[]{:S(2)}) collective-permute-start(bf16[128,3584]{1,0:T(8,128)(2,1)S(1)} %bitcast.40), channel_id=1, source_target_pairs={{0,32},{1,33},{2,34},{3,35},{4,36},{5,37},{6,38},{7,39},{8,40},{9,... | collective-permute-start | bytes 2752520 | tf_op jit(solution)/shard_map/ppermute | solution.py:12
  220.9 16.0 %copy-start.2 = (f32[32,8]{0,1:T(8,128)S(1)}, f32[32,8]{0,1:T(8,128)}, u32[]{:S(2)}) copy-start(f32[32,8]{0,1:T(8,128)} %param.7) | copy-start | bytes 3076
  220.9 182.9 %all-to-all-start.1 = ((bf16[64,4,3584]{2,1,0:T(4,128)(2,1)}), bf16[64,4,3584]{2,1,0:T(4,128)(2,1)S(1)}, u32[]{:S(2)}, u32[]{:S(2)}) async-start(bf16[64,4,3584]{2,1,0:T(4,128)(2,1)} %reshape.73), calls=%async_computation.1 | async-start | bytes 3670016 | tf_op jit(solution)/shard_map/all_to_all | solution.py:62
  236.6 246.6 %reduce-scatter.4.cloned.1.call-start = ((), (), s32[]{:S(2)}) async-start(), calls=%async_computation.3 | async-start | bytes 1949696
Sparse Core Ops, SparseCore 0:
  417.6 65.5 reduce-scatter.3
where the time goes:
time: 498 us; the launch traced here: 492 us
  waiting for transfers between devices  391 us (79%)
  starting transfers between devices  55.4 us (11%)
  matrix products  20.6 us (4%)
  between operations  13.6 us (3%)
  local copies, waits for them, and re-layouts  9.12 us (2%)
    all_to_all x1, waiting for transfers between devices, per_device(): lax.all_to_all(partial_value, 'dp', split_axis=0, concat_axis=0, tiled=True)  166 us
    all_to_all x1, waiting for transfers between devices, per_device(): lax.all_to_all(outgoing, 'dp', split_axis=0, concat_axis=0, tiled=True)  159 us
    unnamed x2, waiting for transfers between devices  65.7 us
    all_to_all x1, starting transfers between devices, per_device(): lax.all_to_all(outgoing, 'dp', split_axis=0, concat_axis=0, tiled=True)  32.1 us
    all_to_all x1, starting transfers between devices, per_device(): lax.all_to_all(partial_value, 'dp', split_axis=0, concat_axis=0, tiled=True)  15.7 us
    dot_general x1, matrix products, per_device(): jnp.einsum('tdc,dcf->tf', selector, weighted, precision=lax.Precision.HIG...  12.9 us
  transfers between devices with their start and end apart: 5, of which 3 were waited for; matrix products, arithmetic and copies ran while one was open for 1% of the time, Pallas kernels for 0%

commit v1 on v0

v1 whole, which is shorter than its diff:
```python
import jax
import jax.numpy as jnp
from jax import lax
from jax.experimental import pallas as pl
from jax.experimental.pallas import tpu as pltpu
from jax.sharding import Mesh, PartitionSpec as P

ROUTE_SCALE = 2.5
AXES = ("xh", "e", "yh", "z")
BF16, F32, I32 = jnp.bfloat16, jnp.float32, jnp.int32
SMEM = pl.BlockSpec(memory_space=pltpu.SMEM)
VMEM = pl.BlockSpec(memory_space=pltpu.VMEM)
PARAMS = pltpu.CompilerParams(vmem_limit_bytes=40 * 2**20)


def matmul(a, b, dims=((1,), (0,))):
    return lax.dot_general(a, b, (dims, ((), ())), preferred_element_type=F32)


def dispatch_kernel(lines, capacity, xh_ref, routes_ref, scores_ref, mine_ref, out_ref, weight_ref):
    tok_rows, top_count = routes_ref.shape
    rows = lines * 2 * capacity
    row = lax.broadcasted_iota(I32, (tok_rows, rows), 1)
    place = row % capacity
    half = row // capacity % 2
    line = row // (2 * capacity)
    expert_at = (half * lines + line) * 2 + xh_ref[0]
    routes = routes_ref[...]
    scores = scores_ref[...]
    scaled = scores / jnp.sum(scores, axis=1, keepdims=True) * ROUTE_SCALE
    weight = jnp.zeros((tok_rows, rows), F32)
    member = jnp.zeros((tok_rows, rows), F32)
    for k in range(top_count):
        match = routes[:, k : k + 1] == expert_at
        member = jnp.where(match, 1.0, member)
        weight = jnp.where(match, scaled[:, k : k + 1], weight)
    before = (
        lax.broadcasted_iota(I32, (tok_rows, tok_rows), 0)
        > lax.broadcasted_iota(I32, (tok_rows, tok_rows), 1)
    ).astype(F32)
    rank = matmul(before.astype(BF16), member.astype(BF16))
    chosen = jnp.where(rank == place.astype(F32), member, 0.0)
    weight = weight * chosen
    high = weight.astype(BF16)
    weight_ref[:tok_rows, :] = high
    weight_ref[tok_rows:, :] = (weight - high.astype(F32)).astype(BF16)
    selector = chosen.astype(BF16)
    for u in range(2):
        out_ref[u] = matmul(selector, mine_ref[u], ((0,), (0,))).astype(BF16)


def spread_kernel(capacity, wants_ref, arrived_ref, out_ref):
    total = arrived_ref.shape[0]
    rows = total // 2
    arrived = arrived_ref[...]
    source = lax.broadcasted_iota(I32, (total, rows), 0)
    row = lax.broadcasted_iota(I32, (total, rows), 1)
    wanted = row // capacity * (2 * capacity) + row % capacity
    picks = []
    for half in range(2):
        pick = (source == wanted + half * capacity).astype(BF16)
        picks.append(matmul(arrived, pick, ((0,), (0,))))
    for p in range(out_ref.shape[0]):
        out_ref[p] = jnp.where(wants_ref[p] == 1, picks[1], picks[0]).astype(BF16)


def mlp_kernel(rows_ref, up_ref, down_ref, out_ref):
    hidden_width = down_ref.shape[1]
    projected = matmul(up_ref[...], rows_ref[...])
    gate = projected[:hidden_width]
    hidden = (gate / (1.0 + jnp.exp(-gate)) * projected[hidden_width:]).astype(BF16)
    step = out_ref.shape[0] // 4
    for c in range(4):
        out_ref[c * step : (c + 1) * step, :] = matmul(
            down_ref[c * step : (c + 1) * step, :], hidden
        ).astype(BF16)


def merge_kernel(capacity, wants_ref, returned_ref, out_ref):
    pieces, part, rows = returned_ref.shape
    sums = [jnp.zeros((part, rows), F32), jnp.zeros((part, rows), F32)]
    for p in range(pieces):
        value = returned_ref[p].astype(F32)
        second = wants_ref[p] == 1
        sums[0] = sums[0] + jnp.where(second, 0.0, value)
        sums[1] = sums[1] + jnp.where(second, value, 0.0)
    target = lax.broadcasted_iota(I32, (2 * rows, rows), 0)
    row = lax.broadcasted_iota(I32, (2 * rows, rows), 1)
    home = row // capacity * (2 * capacity) + row % capacity
    result = jnp.zeros((2 * rows, part), F32)
    for half in range(2):
        put = (target == home + half * capacity).astype(BF16)
        result = result + matmul(put, sums[half].astype(BF16), ((1,), (1,)))
    out_ref[...] = result.astype(BF16)


def combine_kernel(xh_ref, weight_ref, back_ref, kept_ref, sent_ref):
    tok_rows = kept_ref.shape[0]
    for u, ref in ((xh_ref[0], kept_ref), (1 - xh_ref[0], sent_ref)):
        both = matmul(weight_ref[...], back_ref[u])
        ref[...] = both[:tok_rows] + both[tok_rows:]


def shaped(shape, dtype):
    return jax.ShapeDtypeStruct(shape, dtype)


def per_device(tokens, gate_scores, routes, balanced, gate_up, down_proj):
    split = lax.axis_size("e")
    lines = lax.axis_size("z")
    pieces = 2 * split
    tok_rows, top_count = routes.shape
    width = tokens.shape[1]
    part = width // pieces
    hidden_width = down_proj.shape[2]
    expert_count = 2 * 2 * lines
    capacity = min(tok_rows, max(2, 2 * tok_rows * top_count // expert_count))
    rows = 2 * lines * capacity
    xh, e, z = (lax.axis_index(n) for n in ("xh", "e", "z"))
    side = xh.astype(I32).reshape(1)
    near = ("yh", "e")
    far = ("yh", "z")

    mine = jnp.stack(
        [lax.dynamic_slice_in_dim(tokens, (e + u * split) * part, part, 1) for u in range(2)]
    )
    outgoing, weight = pl.pallas_call(
        lambda *refs: dispatch_kernel(lines, capacity, *refs),
        out_shape=(shaped((2, rows, part), BF16), shaped((2 * tok_rows, rows), BF16)),
        in_specs=[SMEM, VMEM, VMEM, VMEM],
        out_specs=(VMEM, VMEM),
        compiler_params=PARAMS,
        name="dispatch",
    )(side, routes, gate_scores, mine)
    outgoing = outgoing.reshape(2 * lines, 2 * capacity, part)
    arrived = lax.all_to_all(outgoing, far, split_axis=0, concat_axis=0, tiled=True)

    own_flag = lax.dynamic_index_in_dim(balanced[:, 0], z, 0, keepdims=True)
    flags = lax.all_gather(own_flag, "e", axis=0, tiled=True)
    wants = jnp.concatenate([flags, 1 - flags])
    spread = pl.pallas_call(
        lambda *refs: spread_kernel(capacity, *refs),
        out_shape=shaped((pieces, part, rows), BF16),
        in_specs=[SMEM, VMEM],
        out_specs=VMEM,
        compiler_params=PARAMS,
        name="spread",
    )(wants, arrived.reshape(2 * rows, part))
    gathered = lax.all_to_all(spread, near, split_axis=0, concat_axis=0, tiled=True)

    partial_value = pl.pallas_call(
        mlp_kernel,
        out_shape=shaped((width, rows), BF16),
        in_specs=[VMEM, VMEM, VMEM],
        out_specs=VMEM,
        compiler_params=PARAMS,
        name="tile_mlp",
    )(gathered.reshape(width, rows), gate_up[0, 0].T, down_proj[0, 0].T)
    returned = lax.all_to_all(
        partial_value.reshape(pieces, part, rows), near, split_axis=0, concat_axis=0, tiled=True
    )

    both = pl.pallas_call(
        lambda *refs: merge_kernel(capacity, *refs),
        out_shape=shaped((2 * rows, part), BF16),
        in_specs=[SMEM, VMEM],
        out_specs=VMEM,
        compiler_params=PARAMS,
        name="merge",
    )(wants, returned)
    both = both.reshape(2 * lines, 2 * capacity, part)
    back = lax.all_to_all(both, far, split_axis=0, concat_axis=0, tiled=True)

    kept, sent = pl.pallas_call(
        combine_kernel,
        out_shape=(shaped((tok_rows, part), F32), shaped((tok_rows, part), F32)),
        in_specs=[SMEM, VMEM, VMEM],
        out_specs=(VMEM, VMEM),
        compiler_params=PARAMS,
        name="combine",
    )(side, weight, back.reshape(2, rows, part))
    return kept + lax.ppermute(sent, "xh", [(0, 1), (1, 0)])


def solution(mesh):
    ep, dp = mesh.shape["ep"], mesh.shape["dp"]
    fine = Mesh(mesh.devices.reshape(2, ep // 2, 2, dp // 2), AXES)
    tok, exp = ("yh", "z"), ("xh", "e")
    placed = (
        P(tok, None),
        P(tok, None),
        P(tok, None),
        P(None, exp),
        P(tok, exp, None, None),
        P(tok, exp, None, None),
    )
    return jax.shard_map(
        per_device, mesh=fine, in_specs=placed, out_specs=P(tok, exp), check_vma=False
    )
```

time: 498 us -> 200 us (0.40); the launches traced: 492 us -> 199 us
  waiting for transfers between devices: 391 us -> 55.8 us
  blocking collectives: 0 us -> 83.7 us
  matrix products: 20.6 us -> 0 us
  starting transfers between devices: 55.4 us -> 39.4 us
  between operations: 13.6 us -> 0.06 us
  Pallas kernels: 0 us -> 7.33 us
    all_to_all x2, waiting for transfers between devices: 325 us -> 51.5 us  [the longest x1 33.7 us: per_device(): lax.all_to_all(outgoing, far, split_axis=0, concat_axis=0, tiled=True)]
    all_to_all x0 -> x2, blocking collectives: none -> 77 us  [the longest x1 49 us: per_device(): back = lax.all_to_all(both, far, split_axis=0, concat_axis=0, tiled=True)]
    unnamed x2 -> x0, waiting for transfers between devices: 65.7 us -> none
    dot_general x5 -> x0, matrix products: 20.6 us -> none  [the longest x1 12.9 us: per_device(): jnp.einsum('tdc,dcf->tf', selector, weighted, precision=lax.Precision.HIG...]
    all_to_all x2, starting transfers between devices: 47.8 us -> 36.3 us  [the longest x1 32 us: per_device(): lax.all_to_all(outgoing, far, split_axis=0, concat_axis=0, tiled=True)]
    unnamed x10 -> x9, local copies, waits for them, and re-layouts: 2.4 us -> 11.3 us
    pallas_call x0 -> x5, Pallas kernels: none -> 7.33 us  [the longest x1 2.3 us: per_device(): pl.pallas_call(lambda *refs: spread_kernel(capacity, *refs), out_shape=sh...]
    all_gather x0 -> x1, blocking collectives: none -> 6.7 us  [per_device(): flags = lax.all_gather(own_flag, 'e', axis=0, tiled=True)]
  transfers between devices with their start and end apart: 5 -> 3, of which waited for: 3 -> 3; matrix products, arithmetic and copies ran while one was open for 1% -> 4% of each run, Pallas kernels for 0% -> 0%
where the time goes in v1:
time: 200 us; the launch traced here: 199 us
  blocking collectives  83.7 us (42%)
  waiting for transfers between devices  55.8 us (28%)
  starting transfers between devices  39.4 us (20%)
  local copies, waits for them, and re-layouts  12.1 us (6%)
  Pallas kernels  7.33 us (4%)
    all_to_all x1, blocking collectives, per_device(): back = lax.all_to_all(both, far, split_axis=0, concat_axis=0, tiled=True)  49 us
    all_to_all x1, waiting for transfers between devices, per_device(): lax.all_to_all(outgoing, far, split_axis=0, concat_axis=0, tiled=True)  33.7 us
    all_to_all x1, starting transfers between devices, per_device(): lax.all_to_all(outgoing, far, split_axis=0, concat_axis=0, tiled=True)  32 us
    all_to_all x1, blocking collectives, per_device(): lax.all_to_all(partial_value.reshape(pieces, part, rows), near, split_axi...  28 us
    all_to_all x1, waiting for transfers between devices, per_device(): lax.all_to_all(spread, near, split_axis=0, concat_axis=0, tiled=True)  17.8 us
    unnamed x9, local copies, waits for them, and re-layouts  11.3 us
    all_gather x1, blocking collectives, per_device(): flags = lax.all_gather(own_flag, 'e', axis=0, tiled=True)  6.7 us
    all_to_all x1, starting transfers between devices, per_device(): lax.all_to_all(spread, near, split_axis=0, concat_axis=0, tiled=True)  4.36 us
  transfers between devices with their start and end apart: 3, of which 3 were waited for; matrix products, arithmetic and copies ran while one was open for 4% of the time, Pallas kernels for 0%

profile of v1, /device:TPU:6, one launch (start us, length us, event | category | flops | bytes accessed | tf_op | source)
XLA Modules:
  0.0 199.1 jit_solution(11075491482955768030)
XLA Ops:
  0.0 0.8 copy.8.refs_2_
  0.8 0.8 copy.7.refs_1_
  1.5 0.8 dynamic-slice_bitcast_fusion.1
  2.4 1.2 dispatch.1
  3.6 32.0 %all-to-all-start = ((bf16[64,8,224]{2,1,0:T(8,128)(2,1)}), bf16[64,8,224]{2,1,0:T(8,128)(2,1)S(1)}, u32[]{:S(2)}, u32[]{:S(2)}) async-start(bf16[64,8,224]{2,1,0:T(8,128)(2,1)} %bitcast.5), calls=%async_computation | async-start | bytes 524288 | tf_op jit(solution)/shard_map/all_to_all | solution.py:136
  35.6 1.3 dynamic-slice.1
  36.9 1.4 bitcast_dynamic-update-slice_fusion
  38.3 6.7 %all-reduce = s32[8]{0:T(128)S(1)} all-reduce(s32[8]{0:T(128)S(1)} %bitcast_dynamic-update-slice_fusion), channel_id=2, replica_groups=mesh['xh'=2,'e'=8,'yh'=2,'z'=32] {'e'}, use_global_device_ids=true, to_apply=%add | all-reduce | flops 8 | bytes 64 | tf_op jit(solution)/shard_map/all_gather | solution.py:139
  45.0 0.1 pad_add_fusion.refs_0_
  45.1 33.7 %all-to-all-done = bf16[64,8,224]{2,1,0:T(8,128)(2,1)S(1)} async-done(((bf16[64,8,224]{2,1,0:T(8,128)(2,1)}), bf16[64,8,224]{2,1,0:T(8,128)(2,1)S(1)}, u32[]{:S(2)}, u32[]{:S(2)}) %all-to-all-start) | async-done | bytes 229408 | tf_op jit(solution)/shard_map/all_to_all | solution.py:136
  78.8 2.3 %spread.1 = bf16[16,224,256]{2,1,0:T(8,128)(2,1)} custom-call(s32[16]{0:T(128)S(1)} %pad_add_fusion.refs_0_, bf16[512,224]{1,0:T(8,128)(2,1)S(1)} %bitcast.24), custom_call_target="tpu_custom_call" | custom-call | tf_op jit(solution)/shard_map/spread/pallas_call | solution.py:141
  81.1 4.4 %all-to-all-start.1 = ((bf16[16,224,256]{2,1,0:T(8,128)(2,1)}), bf16[16,224,256]{2,1,0:T(8,128)(2,1)S(1)}, u32[]{:S(2)}, u32[]{:S(2)}) async-start(bf16[16,224,256]{2,1,0:T(8,128)(2,1)} %spread.1), calls=%async_computation.1 | async-start | bytes 3670016 | tf_op jit(solution)/shard_map/all_to_all | solution.py:149
  85.5 1.6 copy.10
  87.1 3.9 %copy.9 = bf16[1,1,3584,256]{2,3,1,0:T(8,128)(2,1)} copy(bf16[1,1,3584,256]{3,2,1,0:T(8,128)(2,1)} %param.10) | data formatting | bytes 3670016 | tf_op args[4]
  91.0 17.8 %all-to-all-done.1 = bf16[16,224,256]{2,1,0:T(8,128)(2,1)S(1)} async-done(((bf16[16,224,256]{2,1,0:T(8,128)(2,1)}), bf16[16,224,256]{2,1,0:T(8,128)(2,1)S(1)}, u32[]{:S(2)}, u32[]{:S(2)}) %all-to-all-start.1) | async-done | bytes 1835040 | tf_op jit(solution)/shard_map/all_to_all | solution.py:149
  108.8 0.0 copy-start
  108.8 1.5 copy-done
  110.3 2.2 %tile_mlp.1 = bf16[3584,256]{1,0:T(8,128)(2,1)S(1)} custom-call(bf16[3584,256]{1,0:T(8,128)(2,1)S(1)} %bitcast.20, bf16[256,3584]{1,0:T(8,128)(2,1)S(1)} %bitcast.21, bf16[3584,128]{1,0:T(8,128)(2,1)S(1)} %bitcast.23), custom_call_target="tpu_custom_call" | custom-call | tf_op jit(solution)/shard_map/tile_mlp/pallas_call | solution.py:151
  112.4 28.0 %all_to_all.20.refs_1_ = bf16[16,224,256]{2,1,0:T(8,128)(2,1)S(1)} all-to-all(bf16[16,224,256]{2,1,0:T(8,128)(2,1)S(1)} %bitcast.22), channel_id=1, replica_groups=mesh['xh'=2,'e'=8,'yh'=2,'z'=32] {'yh','e'}, dimensions={0} | all-to-all | bytes 3670016 | tf_op jit(solution)/shard_map/all_to_all | solution.py:159
  140.4 1.5 merge.1
  142.0 49.0 %all_to_all.21 = bf16[64,8,224]{2,1,0:T(8,128)(2,1)S(1)} all-to-all(bf16[64,8,224]{2,1,0:T(8,128)(2,1)S(1)} %bitcast.25), channel_id=1, replica_groups=mesh['xh'=2,'e'=8,'yh'=2,'z'=32] {'yh','z'}, dimensions={0} | all-to-all | bytes 458752 | tf_op jit(solution)/shard_map/all_to_all | solution.py:172
  191.0 0.2 combine.1
  191.2 3.0 %collective-permute-start = (f32[32,224]{1,0:T(8,128)S(1)}, f32[32,224]{1,0:T(8,128)S(1)}, u32[]{:S(2)}, u32[]{:S(2)}) collective-permute-start(f32[32,224]{1,0:T(8,128)S(1)} %get-tuple-element.12), channel_id=1, source_target_pairs={{0,512},{512,0},{1,513},{513,1},{2,514},{514,2},{3,515},{515,3},{4... | collective-permute-start | bytes 86024 | tf_op jit(solution)/shard_map/ppermute | solution.py:182
  194.2 4.3 %collective-permute-done = f32[32,224]{1,0:T(8,128)S(1)} collective-permute-done((f32[32,224]{1,0:T(8,128)S(1)}, f32[32,224]{1,0:T(8,128)S(1)}, u32[]{:S(2)}, u32[]{:S(2)}) %collective-permute-start) | collective-permute-done | bytes 28704 | tf_op jit(solution)/shard_map/ppermute | solution.py:182
  198.5 0.6 add.20
  (3 shorter events, 0.0 us)
Async XLA Ops:
  3.6 75.3 %all-to-all-start = ((bf16[64,8,224]{2,1,0:T(8,128)(2,1)}), bf16[64,8,224]{2,1,0:T(8,128)(2,1)S(1)}, u32[]{:S(2)}, u32[]{:S(2)}) async-start(bf16[64,8,224]{2,1,0:T(8,128)(2,1)} %bitcast.5), calls=%async_computation | async-start | bytes 524288 | tf_op jit(solution)/shard_map/all_to_all | solution.py:136
  81.1 27.6 %all-to-all-start.1 = ((bf16[16,224,256]{2,1,0:T(8,128)(2,1)}), bf16[16,224,256]{2,1,0:T(8,128)(2,1)S(1)}, u32[]{:S(2)}, u32[]{:S(2)}) async-start(bf16[16,224,256]{2,1,0:T(8,128)(2,1)} %spread.1), calls=%async_computation.1 | async-start | bytes 3670016 | tf_op jit(solution)/shard_map/all_to_all | solution.py:149
  108.8 1.5 copy-start
  191.2 7.3 %collective-permute-start = (f32[32,224]{1,0:T(8,128)S(1)}, f32[32,224]{1,0:T(8,128)S(1)}, u32[]{:S(2)}, u32[]{:S(2)}) collective-permute-start(f32[32,224]{1,0:T(8,128)S(1)} %get-tuple-element.12), channel_id=1, source_target_pairs={{0,512},{512,0},{1,513},{513,1},{2,514},{514,2},{3,515},{515,3},{4... | collective-permute-start | bytes 86024 | tf_op jit(solution)/shard_map/ppermute | solution.py:182

commit v2 on v0

v2 whole, which is shorter than its diff:
```python
import jax
import jax.numpy as jnp
from jax import lax
from jax.experimental import pallas as pl
from jax.experimental.pallas import tpu as pltpu
from jax.sharding import Mesh, PartitionSpec as P

ROUTE_SCALE = 2.5
AXES = ("xh", "e", "yh", "z")
PLANE = ("yh", "xh", "e")
BF16, F32, I32 = jnp.bfloat16, jnp.float32, jnp.int32
SMEM = pl.BlockSpec(memory_space=pltpu.SMEM)
VMEM = pl.BlockSpec(memory_space=pltpu.VMEM)
PARAMS = pltpu.CompilerParams(vmem_limit_bytes=40 * 2**20)


def matmul(a, b, dims=((1,), (0,))):
    return lax.dot_general(a, b, (dims, ((), ())), preferred_element_type=F32)


def earlier(count):
    return (
        lax.broadcasted_iota(I32, (count, count), 0) > lax.broadcasted_iota(I32, (count, count), 1)
    ).astype(BF16)


def pack_kernel(expert_count, routes_ref, mine_ref, out_ref):
    tok_rows, top_count = routes_ref.shape
    part = mine_ref.shape[1]
    routes = routes_ref[...]
    expert = lax.broadcasted_iota(I32, (tok_rows, expert_count), 1)
    member = jnp.zeros((tok_rows, expert_count), F32)
    for k in range(top_count):
        member = jnp.where(routes[:, k : k + 1] == expert, 1.0, member)
    count = matmul(earlier(tok_rows), member.astype(BF16))
    lane = lax.broadcasted_iota(I32, (tok_rows, out_ref.shape[1] - part), 1)
    extra = jnp.zeros(lane.shape, F32)
    for k in range(top_count):
        named = routes[:, k : k + 1]
        place = jnp.sum(jnp.where(named == expert, count, 0.0), axis=1, keepdims=True)
        extra = jnp.where(lane == k, named.astype(F32), extra)
        extra = jnp.where(lane == top_count + k, place, extra)
    out_ref[...] = jnp.concatenate([mine_ref[...], extra.astype(BF16)], axis=1)


def weight_kernel(lines, capacity, routes_ref, scores_ref, weight_ref):
    tok_rows, top_count = routes_ref.shape
    rows = lines * 4 * capacity
    column = lax.broadcasted_iota(I32, (tok_rows, rows), 1)
    place = column % capacity
    group = column // capacity % 4
    line = column // (4 * capacity)
    expert_at = (group // 2 * lines + line) * 2 + group % 2
    routes = routes_ref[...]
    scores = scores_ref[...]
    scaled = scores / jnp.sum(scores, axis=1, keepdims=True) * ROUTE_SCALE
    weight = jnp.zeros((tok_rows, rows), F32)
    member = jnp.zeros((tok_rows, rows), F32)
    for k in range(top_count):
        match = routes[:, k : k + 1] == expert_at
        member = jnp.where(match, 1.0, member)
        weight = jnp.where(match, scaled[:, k : k + 1], weight)
    rank = matmul(earlier(tok_rows), member.astype(BF16))
    weight = jnp.where(rank == place.astype(F32), weight, 0.0)
    high = weight.astype(BF16)
    weight_ref[:tok_rows, :] = high
    weight_ref[tok_rows:, :] = (weight - high.astype(F32)).astype(BF16)


def spread_kernel(lines, capacity, top_count, z_ref, flags_ref, packed_ref, out_ref):
    count = packed_ref.shape[0]
    tok_rows = count // lines
    columns = out_ref.shape[3]
    part = out_ref.shape[2]
    packed = packed_ref[...]
    extra = packed[:, part : part + 2 * top_count].astype(F32)
    first = (lax.broadcasted_iota(I32, (count, 1), 0) // tok_rows * capacity).astype(F32)
    column = lax.broadcasted_iota(I32, (count, columns), 1).astype(F32)
    picks = []
    for group in range(4):
        expert = ((group // 2 * lines + z_ref[0]) * 2 + group % 2).astype(F32)
        home = jnp.full((count, 1), -1.0, F32)
        for k in range(top_count):
            match = extra[:, k : k + 1] == expert
            home = jnp.where(match, first + extra[:, top_count + k : top_count + k + 1], home)
        picks.append((home == column).astype(BF16))
    rows = matmul(packed[:, :part], jnp.concatenate(picks, axis=1), ((0,), (0,))).astype(BF16)
    rows = [rows[:, g * columns : (g + 1) * columns] for g in range(4)]
    split = out_ref.shape[1] // 2
    for yh in range(2):
        for c in range(2 * split):
            own = flags_ref[c] == 0
            xh = c // split

            @pl.when(own)
            def _(yh=yh, c=c, xh=xh):
                out_ref[yh, c] = rows[2 * yh + xh]

            @pl.when(jnp.logical_not(own))
            def _(yh=yh, c=c, xh=xh):
                out_ref[yh, c] = rows[2 * (1 - yh) + xh]


def mlp_kernel(rows_ref, up_ref, down_ref, out_ref):
    width, hidden_width = down_ref.shape
    columns = rows_ref.shape[2]
    rows = jnp.concatenate([rows_ref[0], rows_ref[1]], axis=1)
    projected = matmul(up_ref[...], rows)
    gate = projected[:hidden_width]
    hidden = (gate / (1.0 + jnp.exp(-gate)) * projected[hidden_width:]).astype(BF16)
    step = width // 4
    for c in range(4):
        here = slice(c * step, (c + 1) * step)
        value = matmul(down_ref[here, :], hidden).astype(BF16)
        out_ref[0, here, :] = value[:, :columns]
        out_ref[1, here, :] = value[:, columns:]


def merge_kernel(capacity, flags_ref, returned_ref, out_ref):
    halves, slots, part, columns = returned_ref.shape
    split = slots // 2
    sums = []
    for group in range(4):
        home, xh = group // 2, group % 2
        total = jnp.zeros((part, columns), F32)
        for c in range(xh * split, (xh + 1) * split):
            source = home ^ flags_ref[c]
            total = total + returned_ref[source, c].astype(F32)
        sums.append(total.astype(BF16))
    target = lax.broadcasted_iota(I32, (4 * columns, 4 * columns), 0)
    held = lax.broadcasted_iota(I32, (4 * columns, 4 * columns), 1)
    group, column = held // columns, held % columns
    home = column // capacity * (4 * capacity) + group * capacity + column % capacity
    put = (target == home).astype(BF16)
    out_ref[...] = matmul(put, jnp.concatenate(sums, axis=1), ((1,), (1,))).astype(BF16)


def combine_kernel(weight_ref, back_ref, mixed_ref):
    tok_rows = mixed_ref.shape[0]
    both = matmul(weight_ref[...], back_ref[...])
    mixed_ref[...] = both[:tok_rows] + both[tok_rows:]


def call(name, kernel, shape, dtype, specs, *args):
    return pl.pallas_call(
        kernel,
        out_shape=jax.ShapeDtypeStruct(shape, dtype),
        in_specs=specs,
        out_specs=VMEM,
        compiler_params=PARAMS,
        name=name,
    )(*args)


def per_device(tokens, gate_scores, routes, balanced, gate_up, down_proj):
    split = lax.axis_size("e")
    lines = lax.axis_size("z")
    slots = 2 * split
    tok_rows, top_count = routes.shape
    width = tokens.shape[1]
    part = width // slots
    expert_count = 4 * lines
    capacity = min(tok_rows, max(2, 2 * tok_rows * top_count // expert_count))
    columns = lines * capacity
    xh, e, z = (lax.axis_index(n) for n in ("xh", "e", "z"))
    packed_width = -(-(part + 2 * top_count) // 128) * 128

    own_flag = lax.dynamic_index_in_dim(balanced[:, 0], z, 0, keepdims=True)
    flags = lax.all_gather(own_flag, ("xh", "e"), axis=0, tiled=True)

    mine = lax.dynamic_slice_in_dim(tokens, (xh * split + e) * part, part, 1)
    packed = call(
        "pack",
        lambda *refs: pack_kernel(expert_count, *refs),
        (tok_rows, packed_width),
        BF16,
        [VMEM, VMEM],
        routes,
        mine,
    )
    packed = lax.all_gather(packed, "z", axis=0, tiled=True)
    spread = call(
        "spread",
        lambda *refs: spread_kernel(lines, capacity, top_count, *refs),
        (2, slots, part, columns),
        BF16,
        [SMEM, SMEM, VMEM],
        z.astype(I32).reshape(1),
        flags,
        packed,
    )
    spread = spread.reshape(2 * slots, part, columns)
    gathered = lax.all_to_all(spread, PLANE, split_axis=0, concat_axis=0, tiled=True)
    partial_value = call(
        "tile_mlp",
        mlp_kernel,
        (2, width, columns),
        BF16,
        [VMEM, VMEM, VMEM],
        gathered.reshape(2, width, columns),
        gate_up[0, 0].T,
        down_proj[0, 0].T,
    )
    partial_value = partial_value.reshape(2 * slots, part, columns)
    returned = lax.all_to_all(partial_value, PLANE, split_axis=0, concat_axis=0, tiled=True)
    merged = call(
        "merge",
        lambda *refs: merge_kernel(capacity, *refs),
        (4 * columns, part),
        BF16,
        [SMEM, VMEM],
        flags,
        returned.reshape(2, slots, part, columns),
    )
    merged = merged.reshape(lines, 4 * capacity, part)
    back = lax.all_to_all(merged, "z", split_axis=0, concat_axis=0, tiled=True)
    weight = call(
        "weight",
        lambda *refs: weight_kernel(lines, capacity, *refs),
        (2 * tok_rows, 4 * columns),
        BF16,
        [VMEM, VMEM],
        routes,
        gate_scores,
    )
    return call(
        "combine",
        combine_kernel,
        (tok_rows, part),
        F32,
        [VMEM, VMEM],
        weight,
        back.reshape(4 * columns, part),
    )


def solution(mesh):
    ep, dp = mesh.shape["ep"], mesh.shape["dp"]
    fine = Mesh(mesh.devices.reshape(2, ep // 2, 2, dp // 2), AXES)
    tok, exp = ("yh", "z"), ("xh", "e")
    placed = (
        P(tok, None),
        P(tok, None),
        P(tok, None),
        P(None, exp),
        P(tok, exp, None, None),
        P(tok, exp, None, None),
    )
    return jax.shard_map(
        per_device, mesh=fine, in_specs=placed, out_specs=P(tok, exp), check_vma=False
    )
```

time: 498 us -> 219 us (0.44)
  waiting for transfers between devices: 391 us -> 62.7 us
  blocking collectives: 0 us -> 110 us
  starting transfers between devices: 55.4 us -> 20.4 us
  matrix products: 20.6 us -> 0 us
  between operations: 13.6 us -> 0.07 us
  Pallas kernels: 0 us -> 11.5 us
    all_to_all x2, waiting for transfers between devices: 325 us -> 62.7 us  [the longest x1 42.4 us: per_device(): back = lax.all_to_all(merged, 'z', split_axis=0, concat_axis=0, tiled=True)]
    all_gather x0 -> x2, blocking collectives: none -> 80.9 us  [the longest x1 70.8 us: per_device(): packed = lax.all_gather(packed, 'z', axis=0, tiled=True)]
    unnamed x2 -> x0, waiting for transfers between devices: 65.7 us -> none
    all_to_all x0 -> x1, blocking collectives: none -> 28.9 us  [per_device(): lax.all_to_all(partial_value, PLANE, split_axis=0, concat_axis=0, tiled=T...]
    all_to_all x2, starting transfers between devices: 47.8 us -> 20.4 us  [the longest x1 13.1 us: per_device(): back = lax.all_to_all(merged, 'z', split_axis=0, concat_axis=0, tiled=True)]
    dot_general x5 -> x0, matrix products: 20.6 us -> none  [the longest x1 12.9 us: per_device(): jnp.einsum('tdc,dcf->tf', selector, weighted, precision=lax.Precision.HIG...]
    pallas_call x0 -> x6, Pallas kernels: none -> 11.5 us  [call(): pl.pallas_call(kernel, out_shape=jax.ShapeDtypeStruct(shape, dtype), in_s...]
    unnamed x10 -> x15, local copies, waits for them, and re-layouts: 2.4 us -> 11.9 us
  transfers between devices with their start and end apart: 5 -> 2, of which waited for: 3 -> 2; matrix products, arithmetic and copies ran while one was open for 1% -> 3% of each run, Pallas kernels for 0% -> 0%
where the time goes in v2:
time: 219 us; the launch traced here: 216 us
  blocking collectives  110 us (50%)
  waiting for transfers between devices  62.7 us (29%)
  starting transfers between devices  20.4 us (9%)
  local copies, waits for them, and re-layouts  12 us (5%)
  Pallas kernels  11.5 us (5%)
    all_gather x1, blocking collectives, per_device(): packed = lax.all_gather(packed, 'z', axis=0, tiled=True)  70.8 us
    all_to_all x1, waiting for transfers between devices, per_device(): back = lax.all_to_all(merged, 'z', split_axis=0, concat_axis=0, tiled=True)  42.4 us
    all_to_all x1, blocking collectives, per_device(): lax.all_to_all(partial_value, PLANE, split_axis=0, concat_axis=0, tiled=T...  28.9 us
    all_to_all x1, waiting for transfers between devices, per_device(): lax.all_to_all(spread, PLANE, split_axis=0, concat_axis=0, tiled=True)  20.3 us
    all_to_all x1, starting transfers between devices, per_device(): back = lax.all_to_all(merged, 'z', split_axis=0, concat_axis=0, tiled=True)  13.1 us
    unnamed x15, local copies, waits for them, and re-layouts  11.9 us
    pallas_call x6, Pallas kernels, call(): pl.pallas_call(kernel, out_shape=jax.ShapeDtypeStruct(shape, dtype), in_s...  11.5 us
    all_gather x1, blocking collectives, per_device(): flags = lax.all_gather(own_flag, ('xh', 'e'), axis=0, tiled=True)  10.1 us
  transfers between devices with their start and end apart: 2, of which 2 were waited for; matrix products, arithmetic and copies ran while one was open for 3% of the time, Pallas kernels for 0%

profile of v2, /device:TPU:6, one launch (start us, length us, event | category | flops | bytes accessed | tf_op | source)
XLA Modules:
  0.0 216.5 jit_solution(5849084970874791165)
XLA Ops:
  0.0 0.0 copy-start
  0.0 0.8 copy.7.refs_0_
  0.8 0.1 copy-done
  1.0 0.1 constant_dynamic-slice_fusion.refs_1_
  1.0 0.4 pack.1
  1.5 70.8 %all_gather.7.refs_2_ = bf16[1024,256]{1,0:T(8,128)(2,1)S(1)} all-gather(bf16[32,256]{1,0:T(8,128)(2,1)S(1)} %pack.1), channel_id=1, replica_groups=mesh['xh'=2,'e'=8,'yh'=2,'z'=32] {'z'}, dimensions={0}, use_global_device_ids=true | all-gather | bytes 540672 | tf_op jit(solution)/shard_map/all_gather | solution.py:181
  72.2 1.3 dynamic-slice.1
  73.5 1.5 bitcast_dynamic-update-slice_fusion
  75.0 10.1 %all-reduce.refs_1_.refs_0_ = s32[16]{0:T(128)S(1)} all-reduce(s32[16]{0:T(128)S(1)} %bitcast_dynamic-update-slice_fusion), channel_id=2, replica_groups=mesh['xh'=2,'e'=8,'yh'=2,'z'=32] {'xh','e'}, use_global_device_ids=true, to_apply=%add | all-reduce | flops 16 | bytes 128 | tf_op jit(solution)/shard_map/all_gather | solution.py:169
  85.1 6.0 %spread.1 = bf16[2,16,224,128]{3,2,1,0:T(8,128)(2,1)S(1)} custom-call(s32[1]{0:T(128)} %bitcast.2.refs_0_, s32[16]{0:T(128)S(1)} %all-reduce.refs_1_.refs_0_, bf16[1024,256]{1,0:T(8,128)(2,1)S(1)} %all_gather.7.refs_2_), custom_call_target="tpu_custom_call" | custom-call | tf_op jit(solution)/shard_map/spread/pallas_call | solution.py:145
  91.1 0.0 copy-start.1
  91.1 1.2 copy-done.1
  92.4 7.3 %all-to-all-start = ((bf16[32,224,128]{2,1,0:T(8,128)(2,1)}), bf16[32,224,128]{2,1,0:T(8,128)(2,1)S(1)}, u32[]{:S(2)}, u32[]{:S(2)}) async-start(bf16[32,224,128]{2,1,0:T(8,128)(2,1)} %bitcast.18), calls=%async_computation | async-start | bytes 3670016 | tf_op jit(solution)/shard_map/all_to_all | solution.py:193
  99.7 3.8 %copy.10 = bf16[1,1,3584,256]{2,3,1,0:T(8,128)(2,1)} copy(bf16[1,1,3584,256]{3,2,1,0:T(8,128)(2,1)} %param.10) | data formatting | bytes 3670016 | tf_op args[4]
  103.6 1.6 copy.11
  105.2 20.3 %all-to-all-done = bf16[32,224,128]{2,1,0:T(8,128)(2,1)S(1)} async-done(((bf16[32,224,128]{2,1,0:T(8,128)(2,1)}), bf16[32,224,128]{2,1,0:T(8,128)(2,1)S(1)}, u32[]{:S(2)}, u32[]{:S(2)}) %all-to-all-start) | async-done | bytes 1835040 | tf_op jit(solution)/shard_map/all_to_all | solution.py:193
  125.5 0.0 copy-start.2
  125.5 1.5 copy-done.2
  127.0 2.2 tile_mlp.1
  129.2 28.9 %all_to_all.15 = bf16[32,224,128]{2,1,0:T(8,128)(2,1)S(1)} all-to-all(bf16[32,224,128]{2,1,0:T(8,128)(2,1)S(1)} %bitcast.20), channel_id=1, replica_groups=mesh['xh'=2,'e'=8,'yh'=2,'z'=32] {'yh','xh','e'}, dimensions={0} | all-to-all | bytes 3670016 | tf_op jit(solution)/shard_map/all_to_all | solution.py:205
  158.0 0.0 copy-start.3
  158.0 1.8 merge.1
  159.8 13.1 %all-to-all-start.2 = ((bf16[32,16,224]{2,1,0:T(8,128)(2,1)}), bf16[32,16,224]{2,1,0:T(8,128)(2,1)S(1)}, u32[]{:S(2)}, u32[]{:S(2)}) async-start(bf16[32,16,224]{2,1,0:T(8,128)(2,1)} %bitcast.11), calls=%async_computation.2 | async-start | bytes 524288 | tf_op jit(solution)/shard_map/all_to_all | solution.py:216
  172.9 0.0 copy-done.3
  172.9 0.1 copy.8.refs_1_
  173.0 0.3 weight.1.weight_ref
  173.3 42.4 %all-to-all-done.2 = bf16[32,16,224]{2,1,0:T(8,128)(2,1)S(1)} async-done(((bf16[32,16,224]{2,1,0:T(8,128)(2,1)}), bf16[32,16,224]{2,1,0:T(8,128)(2,1)S(1)}, u32[]{:S(2)}, u32[]{:S(2)}) %all-to-all-start.2) | async-done | bytes 229408 | tf_op jit(solution)/shard_map/all_to_all | solution.py:216
  215.7 0.8 combine.1
  (1 shorter events, 0.0 us)
Async XLA Ops:
  0.0 1.0 copy-start
  91.1 1.2 copy-start.1
  92.4 33.1 %all-to-all-start = ((bf16[32,224,128]{2,1,0:T(8,128)(2,1)}), bf16[32,224,128]{2,1,0:T(8,128)(2,1)S(1)}, u32[]{:S(2)}, u32[]{:S(2)}) async-start(bf16[32,224,128]{2,1,0:T(8,128)(2,1)} %bitcast.18), calls=%async_computation | async-start | bytes 3670016 | tf_op jit(solution)/shard_map/all_to_all | solution.py:193
  125.5 1.5 copy-start.2
  158.0 14.9 %copy-start.3 = (f32[32,8]{0,1:T(8,128)S(1)}, f32[32,8]{0,1:T(8,128)}, u32[]{:S(2)}) copy-start(f32[32,8]{0,1:T(8,128)} %param.7) | copy-start | bytes 3076
  159.8 55.9 %all-to-all-start.2 = ((bf16[32,16,224]{2,1,0:T(8,128)(2,1)}), bf16[32,16,224]{2,1,0:T(8,128)(2,1)S(1)}, u32[]{:S(2)}, u32[]{:S(2)}) async-start(bf16[32,16,224]{2,1,0:T(8,128)(2,1)} %bitcast.11), calls=%async_computation.2 | async-start | bytes 524288 | tf_op jit(solution)/shard_map/all_to_all | solution.py:216

commit v3 on v2

v3 whole, which is shorter than its diff:
```python
import jax
import jax.numpy as jnp
from jax import lax
from jax.experimental import pallas as pl
from jax.experimental.pallas import tpu as pltpu
from jax.sharding import Mesh, PartitionSpec as P

ROUTE_SCALE = 2.5
AXES = ("xh", "e", "yh", "zh", "zl")
PLANE = ("yh", "xh", "e")
BF16, F32, I32 = jnp.bfloat16, jnp.float32, jnp.int32
SMEM = pl.BlockSpec(memory_space=pltpu.SMEM)
VMEM = pl.BlockSpec(memory_space=pltpu.VMEM)
PARAMS = pltpu.CompilerParams(vmem_limit_bytes=40 * 2**20)


def matmul(a, b, dims=((1,), (0,))):
    return lax.dot_general(a, b, (dims, ((), ())), preferred_element_type=F32)


def pack_kernel(routes_ref, scores_ref, mine_ref, out_ref):
    tok_rows, top_count = routes_ref.shape
    part = mine_ref.shape[1]
    scores = scores_ref[...]
    scaled = scores / jnp.sum(scores, axis=1, keepdims=True) * ROUTE_SCALE
    high = scaled.astype(BF16).astype(F32)
    low = scaled - high
    named = routes_ref[...].astype(F32)
    lane = lax.broadcasted_iota(I32, (tok_rows, out_ref.shape[1] - part), 1)
    extra = jnp.zeros(lane.shape, F32)
    for k in range(top_count):
        extra = jnp.where(lane == k, named[:, k : k + 1], extra)
        extra = jnp.where(lane == top_count + k, high[:, k : k + 1], extra)
        extra = jnp.where(lane == 2 * top_count + k, low[:, k : k + 1], extra)
    out_ref[...] = jnp.concatenate([mine_ref[...], extra.astype(BF16)], axis=1)


def choice(shape, zh, capacity, extra, top_count, with_weight):
    high_lines, low_lines = shape
    lines = high_lines * low_lines
    count = extra.shape[0]
    tok_rows = count // high_lines
    columns = lines * 4 * capacity
    column = lax.broadcasted_iota(I32, (1, columns), 1)
    place = column % capacity
    group = column // capacity % 4
    block = column // (4 * capacity) % high_lines
    low_line = column // (4 * capacity * high_lines)
    expert_at = ((group // 2 * lines + zh * low_lines + low_line) * 2 + group % 2).astype(F32)
    row = lax.broadcasted_iota(I32, (count, 1), 0)
    member = jnp.zeros((count, columns), F32)
    weight = jnp.zeros((count, columns), F32)
    for k in range(top_count):
        match = extra[:, k : k + 1] == expert_at
        member = jnp.where(match, 1.0, member)
        if with_weight:
            scaled = (
                extra[:, top_count + k : top_count + k + 1]
                + extra[:, 2 * top_count + k : 2 * top_count + k + 1]
            )
            weight = jnp.where(match, scaled, weight)
    after = lax.broadcasted_iota(I32, (count, count), 0)
    first = lax.broadcasted_iota(I32, (count, count), 1)
    before = ((after > first) & (after // tok_rows == first // tok_rows)).astype(BF16)
    rank = matmul(before, member.astype(BF16))
    chosen = (rank == place.astype(F32)) & (row // tok_rows == block)
    return jnp.where(chosen, weight if with_weight else member, 0.0)


def select_kernel(shape, capacity, top_count, zh_ref, packed_ref, out_ref):
    part = out_ref.shape[1]
    packed = packed_ref[...]
    extra = packed[:, part : part + 3 * top_count].astype(F32)
    member = choice(shape, zh_ref[0], capacity, extra, top_count, False)
    out_ref[...] = matmul(member.astype(BF16), packed[:, :part], ((0,), (0,))).astype(BF16)


def weight_kernel(shape, capacity, top_count, part, zh_ref, packed_ref, weight_ref):
    count = packed_ref.shape[0]
    extra = packed_ref[:, part : part + 3 * top_count].astype(F32)
    weight = choice(shape, zh_ref[0], capacity, extra, top_count, True)
    high = weight.astype(BF16)
    weight_ref[:count, :] = high
    weight_ref[count:, :] = (weight - high.astype(F32)).astype(BF16)


def spread_kernel(capacity, flags_ref, arrived_ref, out_ref):
    total = arrived_ref.shape[0]
    columns = out_ref.shape[3]
    source = lax.broadcasted_iota(I32, (total, total), 0)
    target = lax.broadcasted_iota(I32, (total, total), 1)
    group, column = target // columns, target % columns
    home = column // capacity * (4 * capacity) + group * capacity + column % capacity
    pick = (source == home).astype(BF16)
    rows = matmul(arrived_ref[...], pick, ((0,), (0,))).astype(BF16)
    rows = [rows[:, g * columns : (g + 1) * columns] for g in range(4)]
    split = out_ref.shape[1] // 2
    for c in range(2 * split):
        xh = c // split
        swap = flags_ref[c]
        out_ref[swap, c] = rows[xh]
        out_ref[1 - swap, c] = rows[2 + xh]


def mlp_kernel(rows_ref, up_ref, down_ref, out_ref):
    width, hidden_width = down_ref.shape
    columns = rows_ref.shape[2]
    rows = jnp.concatenate([rows_ref[0], rows_ref[1]], axis=1)
    projected = matmul(up_ref[...], rows)
    gate = projected[:hidden_width]
    hidden = (gate / (1.0 + jnp.exp(-gate)) * projected[hidden_width:]).astype(BF16)
    step = width // 4
    for c in range(4):
        here = slice(c * step, (c + 1) * step)
        value = matmul(down_ref[here, :], hidden).astype(BF16)
        out_ref[0, here, :] = value[:, :columns]
        out_ref[1, here, :] = value[:, columns:]


def merge_kernel(capacity, flags_ref, returned_ref, out_ref):
    halves, slots, part, columns = returned_ref.shape
    split = slots // 2
    sums = []
    for group in range(4):
        home, xh = group // 2, group % 2
        total = jnp.zeros((part, columns), F32)
        for c in range(xh * split, (xh + 1) * split):
            source = home ^ flags_ref[c]
            total = total + returned_ref[source, c].astype(F32)
        sums.append(total.astype(BF16))
    target = lax.broadcasted_iota(I32, (4 * columns, 4 * columns), 0)
    held = lax.broadcasted_iota(I32, (4 * columns, 4 * columns), 1)
    group, column = held // columns, held % columns
    home = column // capacity * (4 * capacity) + group * capacity + column % capacity
    put = (target == home).astype(BF16)
    out_ref[...] = matmul(put, jnp.concatenate(sums, axis=1), ((1,), (1,))).astype(BF16)


def combine_kernel(weight_ref, back_ref, mixed_ref):
    count = mixed_ref.shape[0]
    both = matmul(weight_ref[...], back_ref[...])
    mixed_ref[...] = (both[:count] + both[count:]).astype(BF16)


def call(name, kernel, shape, dtype, specs, *args):
    return pl.pallas_call(
        kernel,
        out_shape=jax.ShapeDtypeStruct(shape, dtype),
        in_specs=specs,
        out_specs=VMEM,
        compiler_params=PARAMS,
        name=name,
    )(*args)


def per_device(tokens, gate_scores, routes, balanced, gate_up, down_proj):
    split = lax.axis_size("e")
    shape = lax.axis_size("zh"), lax.axis_size("zl")
    lines = shape[0] * shape[1]
    slots = 2 * split
    tok_rows, top_count = routes.shape
    width = tokens.shape[1]
    part = width // slots
    expert_count = 4 * lines
    capacity = min(tok_rows, max(2, 2 * tok_rows * top_count // expert_count))
    columns = lines * capacity
    xh, e, zh, zl = (lax.axis_index(n) for n in ("xh", "e", "zh", "zl"))
    packed_width = -(-(part + 3 * top_count) // 128) * 128
    level = zh.astype(I32).reshape(1)

    mine = lax.dynamic_slice_in_dim(tokens, (xh * split + e) * part, part, 1)
    packed = call(
        "pack",
        pack_kernel,
        (tok_rows, packed_width),
        BF16,
        [VMEM, VMEM, VMEM],
        routes,
        gate_scores,
        mine,
    )
    packed = lax.all_gather(packed, "zh", axis=0, tiled=True)
    outgoing = call(
        "select",
        lambda *refs: select_kernel(shape, capacity, top_count, *refs),
        (4 * columns, part),
        BF16,
        [SMEM, VMEM],
        level,
        packed,
    )
    outgoing = outgoing.reshape(shape[1], 4 * columns // shape[1], part)
    arrived = lax.all_to_all(outgoing, "zl", split_axis=0, concat_axis=0, tiled=True)
    own_flag = lax.dynamic_index_in_dim(
        balanced[:, 0], zh * shape[1] + zl, 0, keepdims=True
    )
    flags = lax.all_gather(own_flag, ("xh", "e"), axis=0, tiled=True)
    weight = call(
        "weight",
        lambda *refs: weight_kernel(shape, capacity, top_count, part, *refs),
        (2 * shape[0] * tok_rows, 4 * columns),
        BF16,
        [SMEM, VMEM],
        level,
        packed,
    )
    spread = call(
        "spread",
        lambda *refs: spread_kernel(capacity, *refs),
        (2, slots, part, columns),
        BF16,
        [SMEM, VMEM],
        flags,
        arrived.reshape(4 * columns, part),
    )
    spread = spread.reshape(2 * slots, part, columns)
    gathered = lax.all_to_all(spread, PLANE, split_axis=0, concat_axis=0, tiled=True)
    partial_value = call(
        "tile_mlp",
        mlp_kernel,
        (2, width, columns),
        BF16,
        [VMEM, VMEM, VMEM],
        gathered.reshape(2, width, columns),
        gate_up[0, 0].T,
        down_proj[0, 0].T,
    )
    partial_value = partial_value.reshape(2 * slots, part, columns)
    returned = lax.all_to_all(partial_value, PLANE, split_axis=0, concat_axis=0, tiled=True)
    merged = call(
        "merge",
        lambda *refs: merge_kernel(capacity, *refs),
        (4 * columns, part),
        BF16,
        [SMEM, VMEM],
        flags,
        returned.reshape(2, slots, part, columns),
    )
    merged = merged.reshape(shape[1], 4 * columns // shape[1], part)
    back = lax.all_to_all(merged, "zl", split_axis=0, concat_axis=0, tiled=True)
    mixed = call(
        "combine",
        combine_kernel,
        (shape[0] * tok_rows, part),
        BF16,
        [VMEM, VMEM],
        weight,
        back.reshape(4 * columns, part),
    )
    mixed = mixed.reshape(shape[0], tok_rows, part)
    mixed = lax.all_to_all(mixed, "zh", split_axis=0, concat_axis=0, tiled=True)
    return jnp.sum(mixed.astype(F32), axis=0)


def solution(mesh):
    ep, dp = mesh.shape["ep"], mesh.shape["dp"]
    low = dp // 8
    fine = Mesh(mesh.devices.reshape(2, ep // 2, 2, dp // 2 // low, low), AXES)
    tok, exp = ("yh", "zh", "zl"), ("xh", "e")
    placed = (
        P(tok, None),
        P(tok, None),
        P(tok, None),
        P(None, exp),
        P(tok, exp, None, None),
        P(tok, exp, None, None),
    )
    return jax.shard_map(
        per_device, mesh=fine, in_specs=placed, out_specs=P(tok, exp), check_vma=False
    )
```

time: 219 us -> 199 us (0.909)
  waiting for transfers between devices: 62.7 us -> 38.5 us
  blocking collectives: 110 us -> 117 us
  Pallas kernels: 11.5 us -> 8.61 us
    all_to_all x0 -> x1, blocking collectives: none -> 34 us  [per_device(): mixed = lax.all_to_all(mixed, 'zh', split_axis=0, concat_axis=0, tiled=True)]
    all_gather x1, blocking collectives: 70.8 us -> 43.8 us  [per_device(): packed = lax.all_gather(packed, 'zh', axis=0, tiled=True)]
    all_to_all x1 -> x2, waiting for transfers between devices: 42.4 us -> 18.2 us  [the longest x1 16.3 us: per_device(): back = lax.all_to_all(merged, 'zl', split_axis=0, concat_axis=0, tiled=True)]
    pallas_call x6 -> x7, Pallas kernels: 11.5 us -> 8.61 us  [call(): pl.pallas_call(kernel, out_shape=jax.ShapeDtypeStruct(shape, dtype), in_s...]
    unnamed x15 -> x11, local copies, waits for them, and re-layouts: 11.9 us -> 11.4 us
    all_to_all x1 -> x2, starting transfers between devices: 13.1 us -> 12.7 us  [the longest x1 7.79 us: per_device(): back = lax.all_to_all(merged, 'zl', split_axis=0, concat_axis=0, tiled=True)]
  transfers between devices with their start and end apart: 2 -> 3, of which waited for: 2 -> 3; matrix products, arithmetic and copies ran while one was open for 3% -> 4% of each run, Pallas kernels for 0% -> 0%
where the time goes in v3:
time: 199 us; the launch traced here: 196 us
  blocking collectives  117 us (59%)
  waiting for transfers between devices  38.5 us (19%)
  starting transfers between devices  20.3 us (10%)
  local copies, waits for them, and re-layouts  11.5 us (6%)
  Pallas kernels  8.61 us (4%)
    all_gather x1, blocking collectives, per_device(): packed = lax.all_gather(packed, 'zh', axis=0, tiled=True)  43.8 us
    all_to_all x1, blocking collectives, per_device(): mixed = lax.all_to_all(mixed, 'zh', split_axis=0, concat_axis=0, tiled=True)  34 us
    all_to_all x1, blocking collectives, per_device(): lax.all_to_all(partial_value, PLANE, split_axis=0, concat_axis=0, tiled=T...  28.9 us
    all_to_all x1, waiting for transfers between devices, per_device(): lax.all_to_all(spread, PLANE, split_axis=0, concat_axis=0, tiled=True)  20.3 us
    all_to_all x1, waiting for transfers between devices, per_device(): back = lax.all_to_all(merged, 'zl', split_axis=0, concat_axis=0, tiled=True)  16.3 us
    unnamed x11, local copies, waits for them, and re-layouts  11.4 us
    all_gather x1, blocking collectives, per_device(): flags = lax.all_gather(own_flag, ('xh', 'e'), axis=0, tiled=True)  10.1 us
    pallas_call x7, Pallas kernels, call(): pl.pallas_call(kernel, out_shape=jax.ShapeDtypeStruct(shape, dtype), in_s...  8.61 us
  transfers between devices with their start and end apart: 3, of which 3 were waited for; matrix products, arithmetic and copies ran while one was open for 4% of the time, Pallas kernels for 0%

profile of v3, /device:TPU:6, one launch (start us, length us, event | category | flops | bytes accessed | tf_op | source)
XLA Modules:
  0.0 196.4 jit_solution(3587970949590612887)
XLA Ops:
  0.0 0.0 copy-start
  0.0 0.8 copy.7.routes_ref
  0.8 0.8 copy.8.scores_ref
  1.6 0.0 copy-done
  1.6 0.1 constant_dynamic-slice_fusion.1.mine_ref
  1.7 0.3 pack.1
  2.0 43.8 %all_gather.6.refs_1_ = bf16[128,256]{1,0:T(8,128)(2,1)S(1)} all-gather(bf16[32,256]{1,0:T(8,128)(2,1)S(1)} %pack.1), channel_id=1, replica_groups=mesh['xh'=2,'e'=8,'yh'=2,'zh'=4,'zl'=8] {'zh'}, dimensions={0}, use_global_device_ids=true | all-gather | bytes 81920 | tf_op jit(solution)/shard_map/all_gather | solution.py:182
  45.8 1.4 select.1
  47.2 5.0 %all-to-all-start = ((bf16[8,64,224]{2,1,0:T(8,128)(2,1)}), bf16[8,64,224]{2,1,0:T(8,128)(2,1)S(1)}, u32[]{:S(2)}, u32[]{:S(2)}) async-start(bf16[8,64,224]{2,1,0:T(8,128)(2,1)} %bitcast.3), calls=%async_computation | async-start | bytes 524288 | tf_op jit(solution)/shard_map/all_to_all | solution.py:193
  52.1 1.3 dynamic-slice.1
  53.5 1.5 bitcast_dynamic-update-slice_fusion
  55.0 10.1 %all-reduce.refs_0_ = s32[16]{0:T(128)S(1)} all-reduce(s32[16]{0:T(128)S(1)} %bitcast_dynamic-update-slice_fusion), channel_id=2, replica_groups=mesh['xh'=2,'e'=8,'yh'=2,'zh'=4,'zl'=8] {'xh','e'}, use_global_device_ids=true, to_apply=%add | all-reduce | flops 16 | bytes 128 | tf_op jit(solution)/shard_map/all_gather | solution.py:197
  65.1 1.9 all-to-all-done
  67.0 2.2 %spread.1 = bf16[2,16,224,128]{3,2,1,0:T(8,128)(2,1)} custom-call(s32[16]{0:T(128)S(1)} %all-reduce.refs_0_, bf16[512,224]{1,0:T(8,128)(2,1)S(1)} %bitcast.24), custom_call_target="tpu_custom_call" | custom-call | tf_op jit(solution)/shard_map/spread/pallas_call | solution.py:146
  69.2 7.6 %all-to-all-start.1 = ((bf16[32,224,128]{2,1,0:T(8,128)(2,1)}), bf16[32,224,128]{2,1,0:T(8,128)(2,1)S(1)}, u32[]{:S(2)}, u32[]{:S(2)}) async-start(bf16[32,224,128]{2,1,0:T(8,128)(2,1)} %bitcast.5), calls=%async_computation.1 | async-start | bytes 3670016 | tf_op jit(solution)/shard_map/all_to_all | solution.py:217
  76.8 3.8 %copy.9 = bf16[1,1,3584,256]{2,3,1,0:T(8,128)(2,1)} copy(bf16[1,1,3584,256]{3,2,1,0:T(8,128)(2,1)} %param.10) | data formatting | bytes 3670016 | tf_op args[4]
  80.6 1.6 copy.10
  82.2 20.3 %all-to-all-done.1 = bf16[32,224,128]{2,1,0:T(8,128)(2,1)S(1)} async-done(((bf16[32,224,128]{2,1,0:T(8,128)(2,1)}), bf16[32,224,128]{2,1,0:T(8,128)(2,1)S(1)}, u32[]{:S(2)}, u32[]{:S(2)}) %all-to-all-start.1) | async-done | bytes 1835040 | tf_op jit(solution)/shard_map/all_to_all | solution.py:217
  102.5 0.0 copy-start.1
  102.5 1.5 copy-done.1
  104.0 2.2 %tile_mlp.1 = bf16[2,3584,128]{2,1,0:T(8,128)(2,1)S(1)} custom-call(bf16[2,3584,128]{2,1,0:T(8,128)(2,1)S(1)} %bitcast.20, bf16[256,3584]{1,0:T(8,128)(2,1)S(1)} %bitcast.21, bf16[3584,128]{1,0:T(8,128)(2,1)S(1)} %bitcast.23), custom_call_target="tpu_custom_call" | custom-call | tf_op jit(solution)/shard_map/tile_mlp/pallas_call | solution.py:146
  106.2 28.9 %all_to_all.25 = bf16[32,224,128]{2,1,0:T(8,128)(2,1)S(1)} all-to-all(bf16[32,224,128]{2,1,0:T(8,128)(2,1)S(1)} %bitcast.22), channel_id=1, replica_groups=mesh['xh'=2,'e'=8,'yh'=2,'zh'=4,'zl'=8] {'yh','xh','e'}, dimensions={0} | all-to-all | bytes 3670016 | tf_op jit(solution)/shard_map/all_to_all | solution.py:229
  135.1 1.7 merge.1
  136.8 7.8 %all-to-all-start.3 = ((bf16[8,64,224]{2,1,0:T(8,128)(2,1)}), bf16[8,64,224]{2,1,0:T(8,128)(2,1)S(1)}, u32[]{:S(2)}, u32[]{:S(2)}) async-start(bf16[8,64,224]{2,1,0:T(8,128)(2,1)} %bitcast.13), calls=%async_computation.3 | async-start | bytes 524288 | tf_op jit(solution)/shard_map/all_to_all | solution.py:240
  144.6 0.6 weight.1.weight_ref
  145.2 16.3 %all-to-all-done.3 = bf16[8,64,224]{2,1,0:T(8,128)(2,1)S(1)} async-done(((bf16[8,64,224]{2,1,0:T(8,128)(2,1)}), bf16[8,64,224]{2,1,0:T(8,128)(2,1)S(1)}, u32[]{:S(2)}, u32[]{:S(2)}) %all-to-all-start.3) | async-done | bytes 229408 | tf_op jit(solution)/shard_map/all_to_all | solution.py:240
  161.5 0.2 combine.1
  161.7 34.0 %all_to_all.26 = bf16[4,32,224]{2,1,0:T(8,128)(2,1)S(1)} all-to-all(bf16[4,32,224]{2,1,0:T(8,128)(2,1)S(1)} %bitcast.26), channel_id=1, replica_groups=mesh['xh'=2,'e'=8,'yh'=2,'zh'=4,'zl'=8] {'zh'}, dimensions={0} | all-to-all | bytes 114688 | tf_op jit(solution)/shard_map/all_to_all | solution.py:251
  195.8 0.6 convert_reduce_fusion
  (1 shorter events, 0.0 us)
Async XLA Ops:
  0.0 1.6 copy-start
  47.2 19.8 %all-to-all-start = ((bf16[8,64,224]{2,1,0:T(8,128)(2,1)}), bf16[8,64,224]{2,1,0:T(8,128)(2,1)S(1)}, u32[]{:S(2)}, u32[]{:S(2)}) async-start(bf16[8,64,224]{2,1,0:T(8,128)(2,1)} %bitcast.3), calls=%async_computation | async-start | bytes 524288 | tf_op jit(solution)/shard_map/all_to_all | solution.py:193
  69.2 33.3 %all-to-all-start.1 = ((bf16[32,224,128]{2,1,0:T(8,128)(2,1)}), bf16[32,224,128]{2,1,0:T(8,128)(2,1)S(1)}, u32[]{:S(2)}, u32[]{:S(2)}) async-start(bf16[32,224,128]{2,1,0:T(8,128)(2,1)} %bitcast.5), calls=%async_computation.1 | async-start | bytes 3670016 | tf_op jit(solution)/shard_map/all_to_all | solution.py:217
  102.5 1.5 copy-start.1
  136.8 24.7 %all-to-all-start.3 = ((bf16[8,64,224]{2,1,0:T(8,128)(2,1)}), bf16[8,64,224]{2,1,0:T(8,128)(2,1)S(1)}, u32[]{:S(2)}, u32[]{:S(2)}) async-start(bf16[8,64,224]{2,1,0:T(8,128)(2,1)} %bitcast.13), calls=%async_computation.3 | async-start | bytes 524288 | tf_op jit(solution)/shard_map/all_to_all | solution.py:240

commit v4 on v2

v4 whole, which is shorter than its diff:
```python
import jax
import jax.numpy as jnp
from jax import lax
from jax.experimental import pallas as pl
from jax.experimental.pallas import tpu as pltpu
from jax.sharding import Mesh, PartitionSpec as P

ROUTE_SCALE = 2.5
CHUNKS = 1
AXES = ("xh", "e", "yh", "z")
PLANE = ("yh", "xh", "e")
BF16, F32, I32 = jnp.bfloat16, jnp.float32, jnp.int32
SMEM = pl.BlockSpec(memory_space=pltpu.SMEM)
VMEM = pl.BlockSpec(memory_space=pltpu.VMEM)
PARAMS = pltpu.CompilerParams(vmem_limit_bytes=24 * 2**20)


def matmul(a, b, dims=((1,), (0,))):
    return lax.dot_general(a, b, (dims, ((), ())), preferred_element_type=F32)


def earlier(count):
    return (
        lax.broadcasted_iota(I32, (count, count), 0) > lax.broadcasted_iota(I32, (count, count), 1)
    ).astype(BF16)


def column_of(lines, capacity, shape):
    column = lax.broadcasted_iota(I32, shape, 1)
    group = column // capacity % 4
    line = column // (4 * capacity)
    return (group // 2 * lines + line) * 2 + group % 2, column % capacity


def dispatch_kernel(lines, capacity, routes_ref, mine_ref, *out_refs):
    top_count, tok_rows = routes_ref.shape
    rows = lines * 4 * capacity
    expert_at, place = column_of(lines, capacity, (1, rows))
    unit = (
        lax.broadcasted_iota(I32, (top_count, top_count), 0)
        == lax.broadcasted_iota(I32, (top_count, top_count), 1)
    ).astype(BF16)
    routes = matmul(routes_ref[...].astype(F32).astype(BF16), unit, ((0,), (0,)))
    member = jnp.zeros((tok_rows, rows), F32)
    for k in range(top_count):
        member = jnp.where(routes[:, k : k + 1] == expert_at.astype(F32), 1.0, member)
    rank = matmul(earlier(tok_rows), member.astype(BF16))
    chosen = jnp.where(rank == place.astype(F32), member, 0.0).astype(BF16)
    value = matmul(chosen, mine_ref[...], ((0,), (0,))).astype(BF16)
    step = value.shape[1] // len(out_refs)
    for h, out_ref in enumerate(out_refs):
        out_ref[...] = value[:, h * step : (h + 1) * step]


def weight_kernel(lines, capacity, routes_ref, scores_ref, weight_ref):
    tok_rows, top_count = routes_ref.shape
    rows = lines * 4 * capacity
    expert_at, place = column_of(lines, capacity, (1, rows))
    routes = routes_ref[...]
    scores = scores_ref[...]
    scaled = scores / jnp.sum(scores, axis=1, keepdims=True) * ROUTE_SCALE
    weight = jnp.zeros((tok_rows, rows), F32)
    member = jnp.zeros((tok_rows, rows), F32)
    for k in range(top_count):
        match = routes[:, k : k + 1] == expert_at
        member = jnp.where(match, 1.0, member)
        weight = jnp.where(match, scaled[:, k : k + 1], weight)
    rank = matmul(earlier(tok_rows), member.astype(BF16))
    weight = jnp.where(rank == place.astype(F32), weight, 0.0)
    high = weight.astype(BF16)
    weight_ref[:tok_rows, :] = high
    weight_ref[tok_rows:, :] = (weight - high.astype(F32)).astype(BF16)


def spread_kernel(capacity, flags_ref, arrived_ref, out_ref):
    total = arrived_ref.shape[0]
    columns = out_ref.shape[3]
    source = lax.broadcasted_iota(I32, (total, total), 0)
    target = lax.broadcasted_iota(I32, (total, total), 1)
    group, column = target // columns, target % columns
    home = column // capacity * (4 * capacity) + group * capacity + column % capacity
    pick = (source == home).astype(BF16)
    rows = matmul(arrived_ref[...], pick, ((0,), (0,))).astype(BF16)
    rows = [rows[:, g * columns : (g + 1) * columns] for g in range(4)]
    split = out_ref.shape[1] // 2
    for c in range(2 * split):
        xh = c // split
        swap = flags_ref[c]
        out_ref[swap, c] = rows[xh]
        out_ref[1 - swap, c] = rows[2 + xh]


def mlp_kernel(chunks, *refs):
    rows_refs, up_refs, down_refs, out_refs = (
        refs[i * chunks : (i + 1) * chunks] for i in range(4)
    )
    hidden_width = down_refs[0].shape[1]
    columns = rows_refs[0].shape[2]
    projected = 0.0
    for rows_ref, up_ref in zip(rows_refs, up_refs):
        rows = jnp.concatenate([rows_ref[0], rows_ref[1]], axis=1)
        projected = projected + matmul(up_ref[...], rows)
    gate = projected[:hidden_width]
    hidden = (gate / (1.0 + jnp.exp(-gate)) * projected[hidden_width:]).astype(BF16)
    for down_ref, out_ref in zip(down_refs, out_refs):
        step = down_ref.shape[0] // 2
        for c in range(2):
            here = slice(c * step, (c + 1) * step)
            value = matmul(down_ref[here, :], hidden).astype(BF16)
            out_ref[0, here, :] = value[:, :columns]
            out_ref[1, here, :] = value[:, columns:]


def merge_kernel(capacity, flags_ref, returned_ref, out_ref):
    halves, slots, part, columns = returned_ref.shape
    split = slots // 2
    sums = []
    for group in range(4):
        home, xh = group // 2, group % 2
        total = jnp.zeros((part, columns), F32)
        for c in range(xh * split, (xh + 1) * split):
            source = home ^ flags_ref[c]
            total = total + returned_ref[source, c].astype(F32)
        sums.append(total.astype(BF16))
    target = lax.broadcasted_iota(I32, (4 * columns, 4 * columns), 0)
    held = lax.broadcasted_iota(I32, (4 * columns, 4 * columns), 1)
    group, column = held // columns, held % columns
    home = column // capacity * (4 * capacity) + group * capacity + column % capacity
    put = (target == home).astype(BF16)
    out_ref[...] = matmul(put, jnp.concatenate(sums, axis=1), ((1,), (1,))).astype(BF16)


def combine_kernel(weight_ref, *refs):
    back_refs, mixed_ref = refs[:-1], refs[-1]
    tok_rows = mixed_ref.shape[0]
    pieces = []
    for back_ref in back_refs:
        both = matmul(weight_ref[...], back_ref[...])
        pieces.append(both[:tok_rows] + both[tok_rows:])
    mixed_ref[...] = jnp.concatenate(pieces, axis=1)


def call(name, kernel, shape, dtype, specs, *args, copies=0):
    one = jax.ShapeDtypeStruct(shape, dtype)
    return pl.pallas_call(
        kernel,
        out_shape=(one,) * copies if copies else one,
        in_specs=specs,
        out_specs=(VMEM,) * copies if copies else VMEM,
        compiler_params=PARAMS,
        name=name,
    )(*args)


def swap(value, axes):
    return lax.all_to_all(value, axes, split_axis=0, concat_axis=0, tiled=True)


def per_device(tokens, gate_scores, routes, balanced, gate_up, down_proj):
    split = lax.axis_size("e")
    lines = lax.axis_size("z")
    slots = 2 * split
    tok_rows, top_count = routes.shape
    width = tokens.shape[1]
    hidden_width = down_proj.shape[2]
    part = width // slots
    step = part // CHUNKS
    expert_count = 4 * lines
    capacity = min(tok_rows, max(2, 2 * tok_rows * top_count // expert_count))
    columns = lines * capacity
    xh, e, z = (lax.axis_index(n) for n in ("xh", "e", "z"))
    every = range(CHUNKS)

    mine = lax.dynamic_slice_in_dim(tokens, (xh * split + e) * part, part, 1)
    outgoing = call(
        "dispatch",
        lambda *refs: dispatch_kernel(lines, capacity, *refs),
        (4 * columns, step),
        BF16,
        [VMEM, VMEM],
        routes.T,
        mine,
        copies=CHUNKS,
    )
    arrived = [swap(v.reshape(lines, 4 * capacity, step), "z") for v in outgoing]
    own_flag = lax.dynamic_index_in_dim(balanced[:, 0], z, 0, keepdims=True)
    flags = lax.all_gather(own_flag, ("xh", "e"), axis=0, tiled=True)
    gathered = []
    for v in arrived:
        spread = call(
            "spread",
            lambda *refs: spread_kernel(capacity, *refs),
            (2, slots, step, columns),
            BF16,
            [SMEM, VMEM],
            flags,
            v.reshape(4 * columns, step),
        )
        v = swap(spread.reshape(2 * slots, step, columns), PLANE)
        gathered.append(v.reshape(2, slots * step, columns))
    up = gate_up[0, 0].reshape(slots, CHUNKS, step, 2 * hidden_width)
    up = [up[:, h].reshape(slots * step, 2 * hidden_width).T for h in every]
    down = down_proj[0, 0].reshape(hidden_width, slots, CHUNKS, step)
    down = [down[:, :, h].reshape(hidden_width, slots * step).T for h in every]
    partial_value = call(
        "tile_mlp",
        lambda *refs: mlp_kernel(CHUNKS, *refs),
        (2, slots * step, columns),
        BF16,
        [VMEM] * (3 * CHUNKS),
        *gathered,
        *up,
        *down,
        copies=CHUNKS,
    )
    back = []
    for v in partial_value:
        returned = swap(v.reshape(2 * slots, step, columns), PLANE)
        merged = call(
            "merge",
            lambda *refs: merge_kernel(capacity, *refs),
            (4 * columns, step),
            BF16,
            [SMEM, VMEM],
            flags,
            returned.reshape(2, slots, step, columns),
        )
        merged = swap(merged.reshape(lines, 4 * capacity, step), "z")
        back.append(merged.reshape(4 * columns, step))
    weight = call(
        "weight",
        lambda *refs: weight_kernel(lines, capacity, *refs),
        (2 * tok_rows, 4 * columns),
        BF16,
        [VMEM, VMEM],
        routes,
        gate_scores,
    )
    return call(
        "combine", combine_kernel, (tok_rows, part), F32, [VMEM] * (1 + CHUNKS), weight, *back
    )


def solution(mesh):
    ep, dp = mesh.shape["ep"], mesh.shape["dp"]
    fine = Mesh(mesh.devices.reshape(2, ep // 2, 2, dp // 2), AXES)
    tok, exp = ("yh", "z"), ("xh", "e")
    placed = (
        P(tok, None),
        P(tok, None),
        P(tok, None),
        P(None, exp),
        P(tok, exp, None, None),
        P(tok, exp, None, None),
    )
    return jax.shard_map(
        per_device, mesh=fine, in_specs=placed, out_specs=P(tok, exp), check_vma=False
    )
```

time: 219 us -> 195 us (0.89)
  blocking collectives: 110 us -> 39 us
  waiting for transfers between devices: 62.7 us -> 92.8 us
  starting transfers between devices: 20.4 us -> 40.2 us
  Pallas kernels: 11.5 us -> 8.56 us
    all_gather x1 -> x0, blocking collectives: 70.8 us -> none  [per_device(): packed = lax.all_gather(packed, 'z', axis=0, tiled=True)]
    all_to_all x2 -> x3, waiting for transfers between devices: 62.7 us -> 92.8 us  [swap(): return lax.all_to_all(value, axes, split_axis=0, concat_axis=0, tiled=True)]
    all_to_all x2 -> x3, starting transfers between devices: 20.4 us -> 40.2 us  [swap(): return lax.all_to_all(value, axes, split_axis=0, concat_axis=0, tiled=True)]
    pallas_call x6, Pallas kernels: 11.5 us -> 8.56 us  [call(): pl.pallas_call(kernel, out_shape=(one,) * copies if copies else one, in_s...]
    unnamed x15 -> x17, local copies, waits for them, and re-layouts: 11.9 us -> 11.5 us
  transfers between devices with their start and end apart: 2 -> 3, of which waited for: 2 -> 3; matrix products, arithmetic and copies ran while one was open for 3% -> 4% of each run, Pallas kernels for 0% -> 0%
where the time goes in v4:
time: 195 us; the launch traced here: 192 us
  waiting for transfers between devices  92.8 us (48%)
  starting transfers between devices  40.2 us (21%)
  blocking collectives  39 us (20%)
  local copies, waits for them, and re-layouts  11.6 us (6%)
  Pallas kernels  8.56 us (4%)
    all_to_all x3, waiting for transfers between devices, swap(): return lax.all_to_all(value, axes, split_axis=0, concat_axis=0, tiled=True)  92.8 us
    all_to_all x3, starting transfers between devices, swap(): return lax.all_to_all(value, axes, split_axis=0, concat_axis=0, tiled=True)  40.2 us
    all_to_all x1, blocking collectives, swap(): return lax.all_to_all(value, axes, split_axis=0, concat_axis=0, tiled=True)  28.9 us
    unnamed x17, local copies, waits for them, and re-layouts  11.5 us
    all_gather x1, blocking collectives, per_device(): flags = lax.all_gather(own_flag, ('xh', 'e'), axis=0, tiled=True)  10.1 us
    pallas_call x6, Pallas kernels, call(): pl.pallas_call(kernel, out_shape=(one,) * copies if copies else one, in_s...  8.56 us
  transfers between devices with their start and end apart: 3, of which 3 were waited for; matrix products, arithmetic and copies ran while one was open for 4% of the time, Pallas kernels for 0%

profile of v4, /device:TPU:6, one launch (start us, length us, event | category | flops | bytes accessed | tf_op | source)
XLA Modules:
  0.0 192.1 jit_solution(15930179385866568616)
XLA Ops:
  0.0 0.0 copy-start
  0.0 0.9 copy-done
  0.9 0.1 constant_dynamic-slice_fusion.refs_1_
  1.0 0.0 copy-start.2
  1.0 0.7 copy-done.2
  1.7 1.4 dispatch.1
  3.1 28.7 %all-to-all-start = ((bf16[32,16,224]{2,1,0:T(8,128)(2,1)}), bf16[32,16,224]{2,1,0:T(8,128)(2,1)S(1)}, u32[]{:S(2)}, u32[]{:S(2)}) async-start(bf16[32,16,224]{2,1,0:T(8,128)(2,1)} %bitcast.3), calls=%async_computation | async-start | bytes 524288 | tf_op jit(solution)/shard_map/all_to_all | solution.py:156
  31.8 1.3 dynamic-slice.1
  33.1 1.5 bitcast_dynamic-update-slice_fusion
  34.6 10.1 %all-reduce.refs_0_ = s32[16]{0:T(128)S(1)} all-reduce(s32[16]{0:T(128)S(1)} %bitcast_dynamic-update-slice_fusion), channel_id=2, replica_groups=mesh['xh'=2,'e'=8,'yh'=2,'z'=32] {'xh','e'}, use_global_device_ids=true, to_apply=%add | all-reduce | flops 16 | bytes 128 | tf_op jit(solution)/shard_map/all_gather | solution.py:187
  44.7 29.7 %all-to-all-done = bf16[32,16,224]{2,1,0:T(8,128)(2,1)S(1)} async-done(((bf16[32,16,224]{2,1,0:T(8,128)(2,1)}), bf16[32,16,224]{2,1,0:T(8,128)(2,1)S(1)}, u32[]{:S(2)}, u32[]{:S(2)}) %all-to-all-start) | async-done | bytes 229408 | tf_op jit(solution)/shard_map/all_to_all | solution.py:156
  74.4 2.2 %spread.1 = bf16[2,16,224,128]{3,2,1,0:T(8,128)(2,1)} custom-call(s32[16]{0:T(128)S(1)} %all-reduce.refs_0_, bf16[512,224]{1,0:T(8,128)(2,1)S(1)} %bitcast.23), custom_call_target="tpu_custom_call" | custom-call | tf_op jit(solution)/shard_map/spread/pallas_call | solution.py:145
  76.6 7.6 %all-to-all-start.1 = ((bf16[32,224,128]{2,1,0:T(8,128)(2,1)}), bf16[32,224,128]{2,1,0:T(8,128)(2,1)S(1)}, u32[]{:S(2)}, u32[]{:S(2)}) async-start(bf16[32,224,128]{2,1,0:T(8,128)(2,1)} %bitcast.5), calls=%async_computation.1 | async-start | bytes 3670016 | tf_op jit(solution)/shard_map/all_to_all | solution.py:156
  84.1 3.9 %copy.9 = bf16[1,1,3584,256]{2,3,1,0:T(8,128)(2,1)} copy(bf16[1,1,3584,256]{3,2,1,0:T(8,128)(2,1)} %param.10) | data formatting | bytes 3670016 | tf_op args[4]
  88.0 1.6 copy.10
  89.6 20.3 %all-to-all-done.1 = bf16[32,224,128]{2,1,0:T(8,128)(2,1)S(1)} async-done(((bf16[32,224,128]{2,1,0:T(8,128)(2,1)}), bf16[32,224,128]{2,1,0:T(8,128)(2,1)S(1)}, u32[]{:S(2)}, u32[]{:S(2)}) %all-to-all-start.1) | async-done | bytes 1835040 | tf_op jit(solution)/shard_map/all_to_all | solution.py:156
  109.9 0.0 copy-start.1
  109.9 1.5 copy-done.1
  111.4 2.2 %tile_mlp.1 = bf16[2,3584,128]{2,1,0:T(8,128)(2,1)S(1)} custom-call(bf16[2,3584,128]{2,1,0:T(8,128)(2,1)S(1)} %bitcast.19, bf16[256,3584]{1,0:T(8,128)(2,1)S(1)} %bitcast.20, bf16[3584,128]{1,0:T(8,128)(2,1)S(1)} %bitcast.22), custom_call_target="tpu_custom_call" | custom-call | tf_op jit(solution)/shard_map/tile_mlp/pallas_call | solution.py:145
  113.6 28.9 %all_to_all.20 = bf16[32,224,128]{2,1,0:T(8,128)(2,1)S(1)} all-to-all(bf16[32,224,128]{2,1,0:T(8,128)(2,1)S(1)} %bitcast.21), channel_id=1, replica_groups=mesh['xh'=2,'e'=8,'yh'=2,'z'=32] {'yh','xh','e'}, dimensions={0} | all-to-all | bytes 3670016 | tf_op jit(solution)/shard_map/all_to_all | solution.py:156
  142.5 0.0 copy-start.3
  142.5 0.0 copy-start.4
  142.5 1.7 merge.1
  144.2 3.9 %all-to-all-start.3 = ((bf16[32,16,224]{2,1,0:T(8,128)(2,1)}), bf16[32,16,224]{2,1,0:T(8,128)(2,1)S(1)}, u32[]{:S(2)}, u32[]{:S(2)}) async-start(bf16[32,16,224]{2,1,0:T(8,128)(2,1)} %bitcast.13), calls=%async_computation.3 | async-start | bytes 524288 | tf_op jit(solution)/shard_map/all_to_all | solution.py:156
  148.1 0.0 copy-done.3
  148.1 0.1 copy.7.refs_0_
  148.2 0.0 copy-done.4
  148.2 0.1 copy.8.refs_1_
  148.3 0.3 weight.1.weight_ref
  148.5 42.8 %all-to-all-done.3 = bf16[32,16,224]{2,1,0:T(8,128)(2,1)S(1)} async-done(((bf16[32,16,224]{2,1,0:T(8,128)(2,1)}), bf16[32,16,224]{2,1,0:T(8,128)(2,1)S(1)}, u32[]{:S(2)}, u32[]{:S(2)}) %all-to-all-start.3) | async-done | bytes 229408 | tf_op jit(solution)/shard_map/all_to_all | solution.py:156
  191.3 0.8 combine.1
  (1 shorter events, 0.0 us)
Async XLA Ops:
  0.0 0.9 copy-start
  1.0 0.7 copy-start.2
  3.1 71.3 %all-to-all-start = ((bf16[32,16,224]{2,1,0:T(8,128)(2,1)}), bf16[32,16,224]{2,1,0:T(8,128)(2,1)S(1)}, u32[]{:S(2)}, u32[]{:S(2)}) async-start(bf16[32,16,224]{2,1,0:T(8,128)(2,1)} %bitcast.3), calls=%async_computation | async-start | bytes 524288 | tf_op jit(solution)/shard_map/all_to_all | solution.py:156
  76.6 33.3 %all-to-all-start.1 = ((bf16[32,224,128]{2,1,0:T(8,128)(2,1)}), bf16[32,224,128]{2,1,0:T(8,128)(2,1)S(1)}, u32[]{:S(2)}, u32[]{:S(2)}) async-start(bf16[32,224,128]{2,1,0:T(8,128)(2,1)} %bitcast.5), calls=%async_computation.1 | async-start | bytes 3670016 | tf_op jit(solution)/shard_map/all_to_all | solution.py:156
  109.9 1.5 copy-start.1
  142.5 5.6 %copy-start.3 = (s32[32,8]{0,1:T(8,128)S(1)}, s32[32,8]{0,1:T(8,128)}, u32[]{:S(2)}) copy-start(s32[32,8]{0,1:T(8,128)} %param.8) | copy-start | bytes 3076
  142.5 5.7 %copy-start.4 = (f32[32,8]{0,1:T(8,128)S(1)}, f32[32,8]{0,1:T(8,128)}, u32[]{:S(2)}) copy-start(f32[32,8]{0,1:T(8,128)} %param.7) | copy-start | bytes 3076
  144.2 47.1 %all-to-all-start.3 = ((bf16[32,16,224]{2,1,0:T(8,128)(2,1)}), bf16[32,16,224]{2,1,0:T(8,128)(2,1)S(1)}, u32[]{:S(2)}, u32[]{:S(2)}) async-start(bf16[32,16,224]{2,1,0:T(8,128)(2,1)} %bitcast.13), calls=%async_computation.3 | async-start | bytes 524288 | tf_op jit(solution)/shard_map/all_to_all | solution.py:156

commit v5 on v4

--- a/solution.py
+++ b/solution.py
@@ -75,8 +75,8 @@
 def spread_kernel(capacity, flags_ref, arrived_ref, out_ref):
     total = arrived_ref.shape[0]
     columns = out_ref.shape[3]
-    source = lax.broadcasted_iota(I32, (total, total), 0)
-    target = lax.broadcasted_iota(I32, (total, total), 1)
+    source = lax.broadcasted_iota(I32, (total, 1), 0)
+    target = lax.broadcasted_iota(I32, (1, total), 1)
     group, column = target // columns, target % columns
     home = column // capacity * (4 * capacity) + group * capacity + column % capacity
     pick = (source == home).astype(BF16)
@@ -122,8 +122,8 @@
             source = home ^ flags_ref[c]
             total = total + returned_ref[source, c].astype(F32)
         sums.append(total.astype(BF16))
-    target = lax.broadcasted_iota(I32, (4 * columns, 4 * columns), 0)
-    held = lax.broadcasted_iota(I32, (4 * columns, 4 * columns), 1)
+    target = lax.broadcasted_iota(I32, (4 * columns, 1), 0)
+    held = lax.broadcasted_iota(I32, (1, 4 * columns), 1)
     group, column = held // columns, held % columns
     home = column // capacity * (4 * capacity) + group * capacity + column % capacity
     put = (target == home).astype(BF16)
@@ -185,6 +185,20 @@
     arrived = [swap(v.reshape(lines, 4 * capacity, step), "z") for v in outgoing]
     own_flag = lax.dynamic_index_in_dim(balanced[:, 0], z, 0, keepdims=True)
     flags = lax.all_gather(own_flag, ("xh", "e"), axis=0, tiled=True)
+    weight = call(
+        "weight",
+        lambda *refs: weight_kernel(lines, capacity, *refs),
+        (2 * tok_rows, 4 * columns),
+        BF16,
+        [VMEM, VMEM],
+        routes,
+        gate_scores,
+    )
+    up = gate_up[0, 0].reshape(slots, CHUNKS, step, 2 * hidden_width)
+    up = [up[:, h].reshape(slots * step, 2 * hidden_width).T for h in every]
+    down = down_proj[0, 0].reshape(hidden_width, slots, CHUNKS, step)
+    down = [down[:, :, h].reshape(hidden_width, slots * step).T for h in every]
+    arrived, up, down, weight = lax.optimization_barrier((arrived, up, down, weight))
     gathered = []
     for v in arrived:
         spread = call(
@@ -198,10 +212,6 @@
         )
         v = swap(spread.reshape(2 * slots, step, columns), PLANE)
         gathered.append(v.reshape(2, slots * step, columns))
-    up = gate_up[0, 0].reshape(slots, CHUNKS, step, 2 * hidden_width)
-    up = [up[:, h].reshape(slots * step, 2 * hidden_width).T for h in every]
-    down = down_proj[0, 0].reshape(hidden_width, slots, CHUNKS, step)
-    down = [down[:, :, h].reshape(hidden_width, slots * step).T for h in every]
     partial_value = call(
         "tile_mlp",
         lambda *refs: mlp_kernel(CHUNKS, *refs),
@@ -227,15 +237,6 @@
         )
         merged = swap(merged.reshape(lines, 4 * capacity, step), "z")
         back.append(merged.reshape(4 * columns, step))
-    weight = call(
-        "weight",
-        lambda *refs: weight_kernel(lines, capacity, *refs),
-        (2 * tok_rows, 4 * columns),
-        BF16,
-        [VMEM, VMEM],
-        routes,
-        gate_scores,
-    )
     return call(
         "combine", combine_kernel, (tok_rows, part), F32, [VMEM] * (1 + CHUNKS), weight, *back
     )

time: 195 us -> 189 us (0.969)
  blocking collectives: 39 us -> 117 us
  waiting for transfers between devices: 92.8 us -> 24.1 us
  starting transfers between devices: 40.2 us -> 28.7 us
  local copies, waits for them, and re-layouts: 11.6 us -> 9.64 us
  Pallas kernels: 8.56 us -> 6.61 us
    all_to_all x1 -> x3, blocking collectives: 28.9 us -> 107 us  [swap(): return lax.all_to_all(value, axes, split_axis=0, concat_axis=0, tiled=True)]
    all_to_all x3 -> x1, waiting for transfers between devices: 92.8 us -> 24.1 us  [swap(): return lax.all_to_all(value, axes, split_axis=0, concat_axis=0, tiled=True)]
    all_to_all x3 -> x1, starting transfers between devices: 40.2 us -> 28.7 us  [swap(): return lax.all_to_all(value, axes, split_axis=0, concat_axis=0, tiled=True)]
    unnamed x17 -> x13, local copies, waits for them, and re-layouts: 11.5 us -> 9.56 us
  transfers between devices with their start and end apart: 3 -> 1, of which waited for: 3 -> 1; matrix products, arithmetic and copies ran while one was open for 4% -> 4% of each run, Pallas kernels for 0% -> 0%
where the time goes in v5:
time: 189 us; the launch traced here: 187 us
  blocking collectives  117 us (62%)
  starting transfers between devices  28.7 us (15%)
  waiting for transfers between devices  24.1 us (13%)
  local copies, waits for them, and re-layouts  9.64 us (5%)
  Pallas kernels  6.61 us (3%)
    all_to_all x3, blocking collectives, swap(): return lax.all_to_all(value, axes, split_axis=0, concat_axis=0, tiled=True)  107 us
    all_to_all x1, starting transfers between devices, swap(): return lax.all_to_all(value, axes, split_axis=0, concat_axis=0, tiled=True)  28.7 us
    all_to_all x1, waiting for transfers between devices, swap(): return lax.all_to_all(value, axes, split_axis=0, concat_axis=0, tiled=True)  24.1 us
    all_gather x1, blocking collectives, per_device(): flags = lax.all_gather(own_flag, ('xh', 'e'), axis=0, tiled=True)  10.1 us
    unnamed x13, local copies, waits for them, and re-layouts  9.56 us
    pallas_call x6, Pallas kernels, call(): pl.pallas_call(kernel, out_shape=(one,) * copies if copies else one, in_s...  6.61 us
  transfers between devices with their start and end apart: 1, of which 1 were waited for; matrix products, arithmetic and copies ran while one was open for 4% of the time, Pallas kernels for 0%

profile of v5, /device:TPU:6, one launch (start us, length us, event | category | flops | bytes accessed | tf_op | source)
XLA Modules:
  0.0 186.5 jit_solution(6343452387542633653)
XLA Ops:
  0.0 0.0 copy-start
  0.0 0.9 copy-done
  0.9 0.1 constant_dynamic-slice_fusion.1.refs_1_
  1.0 0.0 copy-start.1
  1.0 0.7 copy-done.1
  1.7 1.4 dispatch.1
  3.1 28.7 %all-to-all-start = ((bf16[32,16,224]{2,1,0:T(8,128)(2,1)}), bf16[32,16,224]{2,1,0:T(8,128)(2,1)S(1)}, u32[]{:S(2)}, u32[]{:S(2)}) async-start(bf16[32,16,224]{2,1,0:T(8,128)(2,1)} %bitcast.1), calls=%async_computation | async-start | bytes 524288 | tf_op jit(solution)/shard_map/all_to_all | solution.py:156
  31.8 0.8 copy.9.refs_0_
  32.6 0.8 copy.10.refs_1_
  33.4 1.5 copy.8
  34.9 0.0 copy-start.2
  34.9 2.8 %copy.7 = bf16[1,1,3584,256]{2,3,1,0:T(8,128)(2,1)S(1)} copy(bf16[1,1,3584,256]{3,2,1,0:T(8,128)(2,1)} %param.10) | data formatting | bytes 3670016 | tf_op args[4]
  37.7 1.3 dynamic-slice.1
  39.0 0.3 weight.1.weight_ref
  39.3 0.0 copy-done.2
  39.3 0.8 bitcast_dynamic-update-slice_fusion
  40.1 10.1 %all-reduce.refs_0_ = s32[16]{0:T(128)S(1)} all-reduce(s32[16]{0:T(128)S(1)} %bitcast_dynamic-update-slice_fusion), channel_id=2, replica_groups=mesh['xh'=2,'e'=8,'yh'=2,'z'=32] {'xh','e'}, use_global_device_ids=true, to_apply=%add | all-reduce | flops 16 | bytes 128 | tf_op jit(solution)/shard_map/all_gather | solution.py:187
  50.2 24.1 %all-to-all-done = bf16[32,16,224]{2,1,0:T(8,128)(2,1)S(1)} async-done(((bf16[32,16,224]{2,1,0:T(8,128)(2,1)}), bf16[32,16,224]{2,1,0:T(8,128)(2,1)S(1)}, u32[]{:S(2)}, u32[]{:S(2)}) %all-to-all-start) | async-done | bytes 229408 | tf_op jit(solution)/shard_map/all_to_all | solution.py:156
  74.4 1.0 spread.1
  75.3 31.3 %all_to_all.20 = bf16[32,224,128]{2,1,0:T(8,128)(2,1)S(1)} all-to-all(bf16[32,224,128]{2,1,0:T(8,128)(2,1)S(1)} %bitcast.19), channel_id=1, replica_groups=mesh['xh'=2,'e'=8,'yh'=2,'z'=32] {'yh','xh','e'}, dimensions={0} | all-to-all | bytes 3670016 | tf_op jit(solution)/shard_map/all_to_all | solution.py:156
  106.6 2.2 %tile_mlp.1 = bf16[2,3584,128]{2,1,0:T(8,128)(2,1)S(1)} custom-call(bf16[2,3584,128]{2,1,0:T(8,128)(2,1)S(1)} %bitcast.21, bf16[256,3584]{1,0:T(8,128)(2,1)S(1)} %bitcast.20, bf16[3584,128]{1,0:T(8,128)(2,1)S(1)} %bitcast.23), custom_call_target="tpu_custom_call" | custom-call | tf_op jit(solution)/shard_map/tile_mlp/pallas_call | solution.py:145
  108.8 29.7 %all_to_all.21 = bf16[32,224,128]{2,1,0:T(8,128)(2,1)S(1)} all-to-all(bf16[32,224,128]{2,1,0:T(8,128)(2,1)S(1)} %bitcast.22), channel_id=1, replica_groups=mesh['xh'=2,'e'=8,'yh'=2,'z'=32] {'yh','xh','e'}, dimensions={0} | all-to-all | bytes 3670016 | tf_op jit(solution)/shard_map/all_to_all | solution.py:156
  138.4 1.1 merge.1
  139.5 46.2 %all_to_all.22 = bf16[32,16,224]{2,1,0:T(8,128)(2,1)S(1)} all-to-all(bf16[32,16,224]{2,1,0:T(8,128)(2,1)S(1)} %bitcast.25), channel_id=1, replica_groups=mesh['xh'=2,'e'=8,'yh'=2,'z'=32] {'z'}, dimensions={0} | all-to-all | bytes 458752 | tf_op jit(solution)/shard_map/all_to_all | solution.py:156
  185.7 0.8 combine.1
  (1 shorter events, 0.0 us)
Async XLA Ops:
  0.0 0.9 copy-start
  1.0 0.7 copy-start.1
  3.1 71.3 %all-to-all-start = ((bf16[32,16,224]{2,1,0:T(8,128)(2,1)}), bf16[32,16,224]{2,1,0:T(8,128)(2,1)S(1)}, u32[]{:S(2)}, u32[]{:S(2)}) async-start(bf16[32,16,224]{2,1,0:T(8,128)(2,1)} %bitcast.1), calls=%async_computation | async-start | bytes 524288 | tf_op jit(solution)/shard_map/all_to_all | solution.py:156
  34.9 4.4 %copy-start.2 = (s32[64,1]{0,1:T(1,128)S(1)}, s32[64,1]{0,1:T(1,128)}, u32[]{:S(2)}) copy-start(s32[64,1]{0,1:T(1,128)} %param.9) | copy-start | bytes 772

commit v6 on v5

v6 whole, which is shorter than its diff:
```python
import jax
import jax.numpy as jnp
from jax import lax
from jax.experimental import pallas as pl
from jax.experimental.pallas import tpu as pltpu
from jax.sharding import Mesh, PartitionSpec as P

ROUTE_SCALE = 2.5
AXES = ("xh", "e", "yh", "z")
PLANE = ("yh", "xh", "e")
BF16, F32, I32 = jnp.bfloat16, jnp.float32, jnp.int32
SMEM = pl.BlockSpec(memory_space=pltpu.SMEM)
VMEM = pl.BlockSpec(memory_space=pltpu.VMEM)
PARAMS = pltpu.CompilerParams(vmem_limit_bytes=24 * 2**20)


def matmul(a, b, dims=((1,), (0,))):
    return lax.dot_general(a, b, (dims, ((), ())), preferred_element_type=F32)


def earlier(count):
    return (
        lax.broadcasted_iota(I32, (count, count), 0) > lax.broadcasted_iota(I32, (count, count), 1)
    ).astype(BF16)


def column_of(lines, capacity, shape):
    column = lax.broadcasted_iota(I32, shape, 1)
    place = column // (4 * lines)
    line = column // 4 % lines
    group = column % 4
    return (group // 2 * lines + line) * 2 + group % 2, place


def fold(value, shape):
    places = shape[2] // value.shape[1]
    rows = value.shape[0] // places
    wide = [value[p * rows : (p + 1) * rows] for p in range(places)]
    return jnp.concatenate(wide, axis=1).reshape(shape).astype(BF16)


def unfold(value, places):
    lines, groups, width = value.shape
    flat = value.reshape(lines * groups, width)
    part = width // places
    return jnp.concatenate([flat[:, p * part : (p + 1) * part] for p in range(places)], axis=0)


def dispatch_kernel(lines, capacity, routes_ref, mine_ref, out_ref):
    top_count, tok_rows = routes_ref.shape
    rows = lines * 4 * capacity
    expert_at, place = column_of(lines, capacity, (1, rows))
    unit = (
        lax.broadcasted_iota(I32, (top_count, top_count), 0)
        == lax.broadcasted_iota(I32, (top_count, top_count), 1)
    ).astype(BF16)
    routes = matmul(routes_ref[...].astype(F32).astype(BF16), unit, ((0,), (0,)))
    member = jnp.zeros((tok_rows, rows), F32)
    for k in range(top_count):
        member = jnp.where(routes[:, k : k + 1] == expert_at.astype(F32), 1.0, member)
    rank = matmul(earlier(tok_rows), member.astype(BF16))
    chosen = jnp.where(rank == place.astype(F32), member, 0.0).astype(BF16)
    out_ref[...] = fold(matmul(chosen, mine_ref[...], ((0,), (0,))), out_ref.shape)


def weight_kernel(lines, capacity, routes_ref, scores_ref, weight_ref):
    tok_rows, top_count = routes_ref.shape
    rows = lines * 4 * capacity
    expert_at, place = column_of(lines, capacity, (1, rows))
    routes = routes_ref[...]
    scores = scores_ref[...]
    scaled = scores / jnp.sum(scores, axis=1, keepdims=True) * ROUTE_SCALE
    weight = jnp.zeros((tok_rows, rows), F32)
    member = jnp.zeros((tok_rows, rows), F32)
    for k in range(top_count):
        match = routes[:, k : k + 1] == expert_at
        member = jnp.where(match, 1.0, member)
        weight = jnp.where(match, scaled[:, k : k + 1], weight)
    rank = matmul(earlier(tok_rows), member.astype(BF16))
    weight = jnp.where(rank == place.astype(F32), weight, 0.0)
    high = weight.astype(BF16)
    weight_ref[:tok_rows, :] = high
    weight_ref[tok_rows:, :] = (weight - high.astype(F32)).astype(BF16)


def spread_kernel(capacity, flags_ref, arrived_ref, out_ref):
    arrived = unfold(arrived_ref[...], capacity)
    total = arrived.shape[0]
    columns = out_ref.shape[3]
    source = lax.broadcasted_iota(I32, (total, 1), 0)
    target = lax.broadcasted_iota(I32, (1, total), 1)
    pick = (source == target % columns * 4 + target // columns).astype(BF16)
    rows = matmul(arrived, pick, ((0,), (0,))).astype(BF16)
    rows = [rows[:, g * columns : (g + 1) * columns] for g in range(4)]
    split = out_ref.shape[1] // 2
    for c in range(2 * split):
        xh = c // split
        swap = flags_ref[c]
        out_ref[swap, c] = rows[xh]
        out_ref[1 - swap, c] = rows[2 + xh]


def mlp_kernel(rows_ref, up_ref, down_ref, out_ref):
    width, hidden_width = down_ref.shape
    columns = rows_ref.shape[2]
    projected = matmul(up_ref[...], jnp.concatenate([rows_ref[0], rows_ref[1]], axis=1))
    gate = projected[:hidden_width]
    hidden = (gate / (1.0 + jnp.exp(-gate)) * projected[hidden_width:]).astype(BF16)
    step = width // 2
    for c in range(2):
        here = slice(c * step, (c + 1) * step)
        value = matmul(down_ref[here, :], hidden).astype(BF16)
        out_ref[0, here, :] = value[:, :columns]
        out_ref[1, here, :] = value[:, columns:]


def merge_kernel(flags_ref, returned_ref, out_ref):
    halves, slots, part, columns = returned_ref.shape
    split = slots // 2
    sums = []
    for group in range(4):
        home, xh = group // 2, group % 2
        total = jnp.zeros((part, columns), F32)
        for c in range(xh * split, (xh + 1) * split):
            source = home ^ flags_ref[c]
            total = total + returned_ref[source, c].astype(F32)
        sums.append(total.astype(BF16))
    target = lax.broadcasted_iota(I32, (4 * columns, 1), 0)
    held = lax.broadcasted_iota(I32, (1, 4 * columns), 1)
    put = (target == held % columns * 4 + held // columns).astype(BF16)
    out_ref[...] = fold(matmul(put, jnp.concatenate(sums, axis=1), ((1,), (1,))), out_ref.shape)


def combine_kernel(capacity, weight_ref, back_ref, mixed_ref):
    tok_rows = mixed_ref.shape[0]
    both = matmul(weight_ref[...], unfold(back_ref[...], capacity))
    mixed_ref[...] = both[:tok_rows] + both[tok_rows:]


def call(name, kernel, shape, dtype, specs, *args):
    return pl.pallas_call(
        kernel,
        out_shape=jax.ShapeDtypeStruct(shape, dtype),
        in_specs=specs,
        out_specs=VMEM,
        compiler_params=PARAMS,
        name=name,
    )(*args)


def swap(value, axes):
    return lax.all_to_all(value, axes, split_axis=0, concat_axis=0, tiled=True)


def per_device(tokens, gate_scores, routes, balanced, gate_up, down_proj):
    split = lax.axis_size("e")
    lines = lax.axis_size("z")
    slots = 2 * split
    tok_rows, top_count = routes.shape
    width = tokens.shape[1]
    part = width // slots
    expert_count = 4 * lines
    capacity = min(tok_rows, max(2, 2 * tok_rows * top_count // expert_count))
    columns = lines * capacity
    folded = (lines, 4, capacity * part)
    xh, e, z = (lax.axis_index(n) for n in ("xh", "e", "z"))

    mine = lax.dynamic_slice_in_dim(tokens, (xh * split + e) * part, part, 1)
    outgoing = call(
        "dispatch",
        lambda *refs: dispatch_kernel(lines, capacity, *refs),
        folded,
        BF16,
        [VMEM, VMEM],
        routes.T,
        mine,
    )
    arrived = swap(outgoing, "z")

    own_flag = lax.dynamic_index_in_dim(balanced[:, 0], z, 0, keepdims=True)
    flags = lax.all_gather(own_flag, ("xh", "e"), axis=0, tiled=True)
    weight = call(
        "weight",
        lambda *refs: weight_kernel(lines, capacity, *refs),
        (2 * tok_rows, 4 * columns),
        BF16,
        [VMEM, VMEM],
        routes,
        gate_scores,
    )
    up, down = gate_up[0, 0].T, down_proj[0, 0].T
    arrived, up, down, weight = lax.optimization_barrier((arrived, up, down, weight))

    spread = call(
        "spread",
        lambda *refs: spread_kernel(capacity, *refs),
        (2, slots, part, columns),
        BF16,
        [SMEM, VMEM],
        flags,
        arrived,
    )
    gathered = swap(spread.reshape(2 * slots, part, columns), PLANE)
    partial_value = call(
        "tile_mlp",
        mlp_kernel,
        (2, width, columns),
        BF16,
        [VMEM, VMEM, VMEM],
        gathered.reshape(2, width, columns),
        up,
        down,
    )
    returned = swap(partial_value.reshape(2 * slots, part, columns), PLANE)
    merged = call(
        "merge",
        merge_kernel,
        folded,
        BF16,
        [SMEM, VMEM],
        flags,
        returned.reshape(2, slots, part, columns),
    )
    back = swap(merged, "z")
    return call(
        "combine",
        lambda *refs: combine_kernel(capacity, *refs),
        (tok_rows, part),
        F32,
        [VMEM, VMEM],
        weight,
        back,
    )


def solution(mesh):
    ep, dp = mesh.shape["ep"], mesh.shape["dp"]
    fine = Mesh(mesh.devices.reshape(2, ep // 2, 2, dp // 2), AXES)
    tok, exp = ("yh", "z"), ("xh", "e")
    placed = (
        P(tok, None),
        P(tok, None),
        P(tok, None),
        P(None, exp),
        P(tok, exp, None, None),
        P(tok, exp, None, None),
    )
    return jax.shard_map(
        per_device, mesh=fine, in_specs=placed, out_specs=P(tok, exp), check_vma=False
    )
```

time: 189 us -> 184 us (0.974)
  blocking collectives: 117 us -> 114 us
  waiting for transfers between devices: 24.1 us -> 21.2 us
    all_to_all x1, waiting for transfers between devices: 24.1 us -> 21.2 us  [swap(): return lax.all_to_all(value, axes, split_axis=0, concat_axis=0, tiled=True)]
    all_to_all x3, blocking collectives: 107 us -> 104 us  [swap(): return lax.all_to_all(value, axes, split_axis=0, concat_axis=0, tiled=True)]
where the time goes in v6:
time: 184 us; the launch traced here: 181 us
  blocking collectives  114 us (62%)
  starting transfers between devices  28.7 us (16%)
  waiting for transfers between devices  21.2 us (12%)
  local copies, waits for them, and re-layouts  9.64 us (5%)
  Pallas kernels  7.07 us (4%)
    all_to_all x3, blocking collectives, swap(): return lax.all_to_all(value, axes, split_axis=0, concat_axis=0, tiled=True)  104 us
    all_to_all x1, starting transfers between devices, swap(): return lax.all_to_all(value, axes, split_axis=0, concat_axis=0, tiled=True)  28.7 us
    all_to_all x1, waiting for transfers between devices, swap(): return lax.all_to_all(value, axes, split_axis=0, concat_axis=0, tiled=True)  21.2 us
    all_gather x1, blocking collectives, per_device(): flags = lax.all_gather(own_flag, ('xh', 'e'), axis=0, tiled=True)  10.1 us
    unnamed x13, local copies, waits for them, and re-layouts  9.56 us
    pallas_call x6, Pallas kernels, call(): pl.pallas_call(kernel, out_shape=jax.ShapeDtypeStruct(shape, dtype), in_s...  7.07 us
  transfers between devices with their start and end apart: 1, of which 1 were waited for; matrix products, arithmetic and copies ran while one was open for 4% of the time, Pallas kernels for 0%

profile of v6, /device:TPU:6, one launch (start us, length us, event | category | flops | bytes accessed | tf_op | source)
XLA Modules:
  0.0 181.3 jit_solution(2729452723472784001)
XLA Ops:
  0.0 0.0 copy-start
  0.0 0.9 copy-done
  0.9 0.1 constant_dynamic-slice_fusion.1.refs_1_
  1.0 0.0 copy-start.1
  1.0 0.7 copy-done.1
  1.7 1.5 dispatch.1
  3.2 28.7 %all-to-all-start = ((bf16[32,4,896]{2,1,0:T(4,128)(2,1)}), bf16[32,4,896]{2,1,0:T(4,128)(2,1)S(1)}, u32[]{:S(2)}, u32[]{:S(2)}) async-start(bf16[32,4,896]{2,1,0:T(4,128)(2,1)} %dispatch.1), calls=%async_computation | async-start | bytes 458752 | tf_op jit(solution)/shard_map/all_to_all | solution.py:152
  32.0 0.8 copy.9.refs_0_
  32.7 0.8 copy.10.refs_1_
  33.5 1.5 copy.8
  35.0 0.0 copy-start.2
  35.1 2.8 %copy.7 = bf16[1,1,3584,256]{2,3,1,0:T(8,128)(2,1)S(1)} copy(bf16[1,1,3584,256]{3,2,1,0:T(8,128)(2,1)} %param.10) | data formatting | bytes 3670016 | tf_op args[4]
  37.8 1.3 dynamic-slice.1
  39.1 0.3 weight.1.refs_0_
  39.4 0.0 copy-done.2
  39.4 0.8 bitcast_dynamic-update-slice_fusion
  40.2 10.1 %all-reduce.refs_0_.flags_ref = s32[16]{0:T(128)S(1)} all-reduce(s32[16]{0:T(128)S(1)} %bitcast_dynamic-update-slice_fusion), channel_id=2, replica_groups=mesh['xh'=2,'e'=8,'yh'=2,'z'=32] {'xh','e'}, use_global_device_ids=true, to_apply=%add | all-reduce | flops 16 | bytes 128 | tf_op jit(solution)/shard_map/all_gather | solution.py:181
  50.3 21.2 %all-to-all-done.refs_1_ = bf16[32,4,896]{2,1,0:T(4,128)(2,1)S(1)} async-done(((bf16[32,4,896]{2,1,0:T(4,128)(2,1)}), bf16[32,4,896]{2,1,0:T(4,128)(2,1)S(1)}, u32[]{:S(2)}, u32[]{:S(2)}) %all-to-all-start) | async-done | bytes 229408 | tf_op jit(solution)/shard_map/all_to_all | solution.py:152
  71.6 1.1 spread.1
  72.7 31.3 %all_to_all.20 = bf16[32,224,128]{2,1,0:T(8,128)(2,1)S(1)} all-to-all(bf16[32,224,128]{2,1,0:T(8,128)(2,1)S(1)} %bitcast.15), channel_id=1, replica_groups=mesh['xh'=2,'e'=8,'yh'=2,'z'=32] {'yh','xh','e'}, dimensions={0} | all-to-all | bytes 3670016 | tf_op jit(solution)/shard_map/all_to_all | solution.py:152
  104.0 2.2 %tile_mlp.1 = bf16[2,3584,128]{2,1,0:T(8,128)(2,1)S(1)} custom-call(bf16[2,3584,128]{2,1,0:T(8,128)(2,1)S(1)} %bitcast.17, bf16[256,3584]{1,0:T(8,128)(2,1)S(1)} %bitcast.16, bf16[3584,128]{1,0:T(8,128)(2,1)S(1)} %bitcast.19), custom_call_target="tpu_custom_call" | custom-call | tf_op jit(solution)/shard_map/tile_mlp/pallas_call | solution.py:141
  106.1 29.7 %all_to_all.21 = bf16[32,224,128]{2,1,0:T(8,128)(2,1)S(1)} all-to-all(bf16[32,224,128]{2,1,0:T(8,128)(2,1)S(1)} %bitcast.18), channel_id=1, replica_groups=mesh['xh'=2,'e'=8,'yh'=2,'z'=32] {'yh','xh','e'}, dimensions={0} | all-to-all | bytes 3670016 | tf_op jit(solution)/shard_map/all_to_all | solution.py:152
  135.8 1.1 merge.1
  136.9 43.4 %all_to_all.22.refs_1_ = bf16[32,4,896]{2,1,0:T(4,128)(2,1)S(1)} all-to-all(bf16[32,4,896]{2,1,0:T(4,128)(2,1)S(1)} %merge.1), channel_id=1, replica_groups=mesh['xh'=2,'e'=8,'yh'=2,'z'=32] {'z'}, dimensions={0} | all-to-all | bytes 458752 | tf_op jit(solution)/shard_map/all_to_all | solution.py:152
  180.4 0.9 combine.1
  (1 shorter events, 0.0 us)
Async XLA Ops:
  0.0 0.9 copy-start
  1.0 0.7 copy-start.1
  3.2 68.4 %all-to-all-start = ((bf16[32,4,896]{2,1,0:T(4,128)(2,1)}), bf16[32,4,896]{2,1,0:T(4,128)(2,1)S(1)}, u32[]{:S(2)}, u32[]{:S(2)}) async-start(bf16[32,4,896]{2,1,0:T(4,128)(2,1)} %dispatch.1), calls=%async_computation | async-start | bytes 458752 | tf_op jit(solution)/shard_map/all_to_all | solution.py:152
  35.0 4.4 %copy-start.2 = (s32[64,1]{0,1:T(1,128)S(1)}, s32[64,1]{0,1:T(1,128)}, u32[]{:S(2)}) copy-start(s32[64,1]{0,1:T(1,128)} %param.9) | copy-start | bytes 772

commit v7 on v6

--- a/solution.py
+++ b/solution.py
@@ -27,7 +27,7 @@
 def column_of(lines, capacity, shape):
     column = lax.broadcasted_iota(I32, shape, 1)
     place = column // (4 * lines)
-    line = column // 4 % lines
+    line = (column // 4 + lines // 2) % lines
     group = column % 4
     return (group // 2 * lines + line) * 2 + group % 2, place
 
@@ -149,7 +149,13 @@
 
 
 def swap(value, axes):
-    return lax.all_to_all(value, axes, split_axis=0, concat_axis=0, tiled=True)
+    order = None
+    if axes == "z":
+        lines = lax.axis_size("z")
+        order = [[(z + lines // 2) % lines for z in range(lines)]]
+    return lax.all_to_all(
+        value, axes, split_axis=0, concat_axis=0, axis_index_groups=order, tiled=True
+    )
 
 
 def per_device(tokens, gate_scores, routes, balanced, gate_up, down_proj):

time: 184 us -> 172 us (0.935)
  waiting for transfers between devices: 21.2 us -> 1.66 us
  starting transfers between devices: 28.7 us -> 35.9 us
    all_to_all x1, waiting for transfers between devices: 21.2 us -> 1.66 us  [swap(): lax.all_to_all(value, axes, split_axis=0, concat_axis=0, axis_index_group...]
    all_to_all x1, starting transfers between devices: 28.7 us -> 35.9 us  [swap(): lax.all_to_all(value, axes, split_axis=0, concat_axis=0, axis_index_group...]
  transfers between devices with their start and end apart: 1 -> 1, of which waited for: 1 -> 1; matrix products, arithmetic and copies ran while one was open for 4% -> 5% of each run, Pallas kernels for 0% -> 0%
where the time goes in v7:
time: 172 us; the launch traced here: 169 us
  blocking collectives  114 us (66%)
  starting transfers between devices  35.9 us (21%)
  local copies, waits for them, and re-layouts  9.64 us (6%)
  Pallas kernels  7.08 us (4%)
    all_to_all x3, blocking collectives, swap(): lax.all_to_all(value, axes, split_axis=0, concat_axis=0, axis_index_group...  104 us
    all_to_all x1, starting transfers between devices, swap(): lax.all_to_all(value, axes, split_axis=0, concat_axis=0, axis_index_group...  35.9 us
    all_gather x1, blocking collectives, per_device(): flags = lax.all_gather(own_flag, ('xh', 'e'), axis=0, tiled=True)  10.1 us
    unnamed x13, local copies, waits for them, and re-layouts  9.56 us
    pallas_call x6, Pallas kernels, call(): pl.pallas_call(kernel, out_shape=jax.ShapeDtypeStruct(shape, dtype), in_s...  7.08 us
  transfers between devices with their start and end apart: 1, of which 1 were waited for; matrix products, arithmetic and copies ran while one was open for 5% of the time, Pallas kernels for 0%

profile of v7, /device:TPU:6, one launch (start us, length us, event | category | flops | bytes accessed | tf_op | source)
XLA Modules:
  0.0 168.9 jit_solution(14110883153404394011)
XLA Ops:
  0.0 0.0 copy-start
  0.0 0.9 copy-done
  0.9 0.1 constant_dynamic-slice_fusion.1.refs_1_
  1.0 0.0 copy-start.1
  1.0 0.7 copy-done.1
  1.7 1.5 dispatch.1
  3.2 35.9 %all-to-all-start = ((bf16[32,4,896]{2,1,0:T(4,128)(2,1)}), bf16[32,4,896]{2,1,0:T(4,128)(2,1)S(1)}, u32[]{:S(2)}, u32[]{:S(2)}) async-start(bf16[32,4,896]{2,1,0:T(4,128)(2,1)} %dispatch.1), calls=%async_computation | async-start | bytes 458752 | tf_op jit(solution)/shard_map/all_to_all | solution.py:156
  39.1 0.8 copy.9.refs_0_
  39.9 0.8 copy.10.refs_1_
  40.6 1.5 copy.8
  42.2 0.0 copy-start.2
  42.2 2.8 %copy.7 = bf16[1,1,3584,256]{2,3,1,0:T(8,128)(2,1)S(1)} copy(bf16[1,1,3584,256]{3,2,1,0:T(8,128)(2,1)} %param.10) | data formatting | bytes 3670016 | tf_op args[4]
  45.0 1.3 dynamic-slice.1
  46.2 0.3 weight.1.refs_0_
  46.5 0.0 copy-done.2
  46.6 0.8 bitcast_dynamic-update-slice_fusion
  47.4 10.1 %all-reduce.refs_0_.flags_ref = s32[16]{0:T(128)S(1)} all-reduce(s32[16]{0:T(128)S(1)} %bitcast_dynamic-update-slice_fusion), channel_id=2, replica_groups=mesh['xh'=2,'e'=8,'yh'=2,'z'=32] {'xh','e'}, use_global_device_ids=true, to_apply=%add | all-reduce | flops 16 | bytes 128 | tf_op jit(solution)/shard_map/all_gather | solution.py:187
  57.5 1.7 all-to-all-done.refs_1_
  59.2 1.1 spread.1
  60.3 31.3 %all_to_all.20 = bf16[32,224,128]{2,1,0:T(8,128)(2,1)S(1)} all-to-all(bf16[32,224,128]{2,1,0:T(8,128)(2,1)S(1)} %bitcast.15), channel_id=1, replica_groups=mesh['xh'=2,'e'=8,'yh'=2,'z'=32] {'yh','xh','e'}, dimensions={0} | all-to-all | bytes 3670016 | tf_op jit(solution)/shard_map/all_to_all | solution.py:156
  91.6 2.2 %tile_mlp.1 = bf16[2,3584,128]{2,1,0:T(8,128)(2,1)S(1)} custom-call(bf16[2,3584,128]{2,1,0:T(8,128)(2,1)S(1)} %bitcast.17, bf16[256,3584]{1,0:T(8,128)(2,1)S(1)} %bitcast.16, bf16[3584,128]{1,0:T(8,128)(2,1)S(1)} %bitcast.19), custom_call_target="tpu_custom_call" | custom-call | tf_op jit(solution)/shard_map/tile_mlp/pallas_call | solution.py:141
  93.7 29.7 %all_to_all.21 = bf16[32,224,128]{2,1,0:T(8,128)(2,1)S(1)} all-to-all(bf16[32,224,128]{2,1,0:T(8,128)(2,1)S(1)} %bitcast.18), channel_id=1, replica_groups=mesh['xh'=2,'e'=8,'yh'=2,'z'=32] {'yh','xh','e'}, dimensions={0} | all-to-all | bytes 3670016 | tf_op jit(solution)/shard_map/all_to_all | solution.py:156
  123.4 1.1 merge.1
  124.5 43.4 %all_to_all.22.refs_1_ = bf16[32,4,896]{2,1,0:T(4,128)(2,1)S(1)} all-to-all(bf16[32,4,896]{2,1,0:T(4,128)(2,1)S(1)} %merge.1), channel_id=1, replica_groups={{16,17,18,19,20,21,22,23,24,25,26,27,28,29,30,31,0,1,2,3,4,5,6,7,8,9,10..., dimensions={0} | all-to-all | bytes 458752 | tf_op jit(solution)/shard_map/all_to_all | solution.py:156
  168.0 0.9 combine.1
  (1 shorter events, 0.0 us)
Async XLA Ops:
  0.0 0.9 copy-start
  1.0 0.7 copy-start.1
  3.2 55.9 %all-to-all-start = ((bf16[32,4,896]{2,1,0:T(4,128)(2,1)}), bf16[32,4,896]{2,1,0:T(4,128)(2,1)S(1)}, u32[]{:S(2)}, u32[]{:S(2)}) async-start(bf16[32,4,896]{2,1,0:T(4,128)(2,1)} %dispatch.1), calls=%async_computation | async-start | bytes 458752 | tf_op jit(solution)/shard_map/all_to_all | solution.py:156
  42.2 4.4 %copy-start.2 = (s32[64,1]{0,1:T(1,128)S(1)}, s32[64,1]{0,1:T(1,128)}, u32[]{:S(2)}) copy-start(s32[64,1]{0,1:T(1,128)} %param.9) | copy-start | bytes 772

commit v8 on v7

--- a/solution.py
+++ b/solution.py
@@ -11,7 +11,7 @@
 BF16, F32, I32 = jnp.bfloat16, jnp.float32, jnp.int32
 SMEM = pl.BlockSpec(memory_space=pltpu.SMEM)
 VMEM = pl.BlockSpec(memory_space=pltpu.VMEM)
-PARAMS = pltpu.CompilerParams(vmem_limit_bytes=24 * 2**20)
+HBM = pl.BlockSpec(memory_space=pltpu.HBM)
 
 
 def matmul(a, b, dims=((1,), (0,))):
@@ -46,7 +46,17 @@
     return jnp.concatenate([flat[:, p * part : (p + 1) * part] for p in range(places)], axis=0)
 
 
-def dispatch_kernel(lines, capacity, routes_ref, mine_ref, out_ref):
+def dispatch_kernel(
+    lines, capacity, part, start_ref, routes_hbm, tokens_hbm, out_ref, routes_ref, window_ref, sems
+):
+    window = window_ref.shape[1]
+    base = jnp.minimum(start_ref[0] // 128 * 128, tokens_hbm.shape[1] - window)
+    here = pl.ds(pl.multiple_of(base, 128), window)
+    fetch_routes = pltpu.make_async_copy(routes_hbm, routes_ref, sems.at[0])
+    fetch_tokens = pltpu.make_async_copy(tokens_hbm.at[:, here], window_ref, sems.at[1])
+    fetch_routes.start()
+    fetch_tokens.start()
+    fetch_routes.wait()
     top_count, tok_rows = routes_ref.shape
     rows = lines * 4 * capacity
     expert_at, place = column_of(lines, capacity, (1, rows))
@@ -60,7 +70,10 @@
         member = jnp.where(routes[:, k : k + 1] == expert_at.astype(F32), 1.0, member)
     rank = matmul(earlier(tok_rows), member.astype(BF16))
     chosen = jnp.where(rank == place.astype(F32), member, 0.0).astype(BF16)
-    out_ref[...] = fold(matmul(chosen, mine_ref[...], ((0,), (0,))), out_ref.shape)
+    fetch_tokens.wait()
+    shift = lax.rem(window - (start_ref[0] - base), window)
+    mine = pltpu.roll(window_ref[...].astype(F32), shift, 1)[:, :part].astype(BF16)
+    out_ref[...] = fold(matmul(chosen, mine, ((0,), (0,))), out_ref.shape)
 
 
 def weight_kernel(lines, capacity, routes_ref, scores_ref, weight_ref):
@@ -137,13 +150,14 @@
     mixed_ref[...] = both[:tok_rows] + both[tok_rows:]
 
 
-def call(name, kernel, shape, dtype, specs, *args):
+def call(name, kernel, shape, dtype, specs, *args, scratch=(), limit=24):
     return pl.pallas_call(
         kernel,
         out_shape=jax.ShapeDtypeStruct(shape, dtype),
         in_specs=specs,
         out_specs=VMEM,
-        compiler_params=PARAMS,
+        scratch_shapes=scratch,
+        compiler_params=pltpu.CompilerParams(vmem_limit_bytes=limit * 2**20),
         name=name,
     )(*args)
 
@@ -171,15 +185,23 @@
     folded = (lines, 4, capacity * part)
     xh, e, z = (lax.axis_index(n) for n in ("xh", "e", "z"))
 
-    mine = lax.dynamic_slice_in_dim(tokens, (xh * split + e) * part, part, 1)
+    start = ((xh * split + e) * part).astype(I32).reshape(1)
+    window = -(-(part + 127) // 128) * 128
     outgoing = call(
         "dispatch",
-        lambda *refs: dispatch_kernel(lines, capacity, *refs),
+        lambda *refs: dispatch_kernel(lines, capacity, part, *refs),
         folded,
         BF16,
-        [VMEM, VMEM],
+        [SMEM, HBM, HBM],
+        start,
         routes.T,
-        mine,
+        tokens,
+        limit=63,
+        scratch=[
+            pltpu.VMEM((top_count, tok_rows), I32),
+            pltpu.VMEM((tok_rows, window), BF16),
+            pltpu.SemaphoreType.DMA((2,)),
+        ],
     )
     arrived = swap(outgoing, "z")
 

time: 172 us -> 171 us (level)
    unnamed x13 -> x9, local copies, waits for them, and re-layouts: 9.56 us -> 7.93 us
where the time goes in v8:
time: 171 us; the launch traced here: 168 us
  blocking collectives  114 us (67%)
  starting transfers between devices  35.9 us (21%)
  local copies, waits for them, and re-layouts  7.93 us (5%)
  Pallas kernels  7.8 us (5%)
    all_to_all x3, blocking collectives, swap(): lax.all_to_all(value, axes, split_axis=0, concat_axis=0, axis_index_group...  104 us
    all_to_all x1, starting transfers between devices, swap(): lax.all_to_all(value, axes, split_axis=0, concat_axis=0, axis_index_group...  35.9 us
    all_gather x1, blocking collectives, per_device(): flags = lax.all_gather(own_flag, ('xh', 'e'), axis=0, tiled=True)  10.1 us
    unnamed x9, local copies, waits for them, and re-layouts  7.93 us
    pallas_call x6, Pallas kernels, call(): pl.pallas_call(kernel, out_shape=jax.ShapeDtypeStruct(shape, dtype), in_s...  7.8 us
  transfers between devices with their start and end apart: 1, of which 1 were waited for; matrix products, arithmetic and copies ran while one was open for 5% of the time, Pallas kernels for 0%

profile of v8, /device:TPU:6, one launch (start us, length us, event | category | flops | bytes accessed | tf_op | source)
XLA Modules:
  0.0 167.9 jit_solution(12928977461434806420)
XLA Ops:
  0.0 2.2 %dispatch.1 = bf16[32,4,896]{2,1,0:T(4,128)(2,1)} custom-call(s32[1]{0:T(128)} %bitcast.refs_0_, s32[8,32]{1,0:T(8,128)} %bitcast.21, bf16[32,3584]{1,0:T(8,128)(2,1)} %refs_2_.1), custom_call_target="tpu_custom_call" | custom-call | tf_op jit(solution)/shard_map/dispatch/pallas_call | solution.py:154
  2.2 35.9 %all-to-all-start = ((bf16[32,4,896]{2,1,0:T(4,128)(2,1)}), bf16[32,4,896]{2,1,0:T(4,128)(2,1)S(1)}, u32[]{:S(2)}, u32[]{:S(2)}) async-start(bf16[32,4,896]{2,1,0:T(4,128)(2,1)} %dispatch.1), calls=%async_computation | async-start | bytes 458752 | tf_op jit(solution)/shard_map/all_to_all | solution.py:170
  38.1 0.8 copy.9.refs_0_
  38.9 0.8 copy.10.refs_1_
  39.7 1.5 copy.8
  41.2 0.0 copy-start
  41.2 2.8 %copy.7 = bf16[1,1,3584,256]{2,3,1,0:T(8,128)(2,1)S(1)} copy(bf16[1,1,3584,256]{3,2,1,0:T(8,128)(2,1)} %param.10) | data formatting | bytes 3670016 | tf_op args[4]
  44.0 1.3 dynamic-slice.1
  45.3 0.3 weight.1.refs_0_
  45.6 0.0 copy-done
  45.6 0.8 bitcast_dynamic-update-slice_fusion
  46.4 10.1 %all-reduce.refs_0_.flags_ref = s32[16]{0:T(128)S(1)} all-reduce(s32[16]{0:T(128)S(1)} %bitcast_dynamic-update-slice_fusion), channel_id=2, replica_groups=mesh['xh'=2,'e'=8,'yh'=2,'z'=32] {'xh','e'}, use_global_device_ids=true, to_apply=%add | all-reduce | flops 16 | bytes 128 | tf_op jit(solution)/shard_map/all_gather | solution.py:209
  56.5 1.7 all-to-all-done.refs_1_
  58.2 1.1 spread.1
  59.3 31.3 %all_to_all.20 = bf16[32,224,128]{2,1,0:T(8,128)(2,1)S(1)} all-to-all(bf16[32,224,128]{2,1,0:T(8,128)(2,1)S(1)} %bitcast.16), channel_id=1, replica_groups=mesh['xh'=2,'e'=8,'yh'=2,'z'=32] {'yh','xh','e'}, dimensions={0} | all-to-all | bytes 3670016 | tf_op jit(solution)/shard_map/all_to_all | solution.py:170
  90.6 2.2 %tile_mlp.1 = bf16[2,3584,128]{2,1,0:T(8,128)(2,1)S(1)} custom-call(bf16[2,3584,128]{2,1,0:T(8,128)(2,1)S(1)} %bitcast.18, bf16[256,3584]{1,0:T(8,128)(2,1)S(1)} %bitcast.17, bf16[3584,128]{1,0:T(8,128)(2,1)S(1)} %bitcast.20), custom_call_target="tpu_custom_call" | custom-call | tf_op jit(solution)/shard_map/tile_mlp/pallas_call | solution.py:154
  92.8 29.7 %all_to_all.21 = bf16[32,224,128]{2,1,0:T(8,128)(2,1)S(1)} all-to-all(bf16[32,224,128]{2,1,0:T(8,128)(2,1)S(1)} %bitcast.19), channel_id=1, replica_groups=mesh['xh'=2,'e'=8,'yh'=2,'z'=32] {'yh','xh','e'}, dimensions={0} | all-to-all | bytes 3670016 | tf_op jit(solution)/shard_map/all_to_all | solution.py:170
  122.4 1.1 merge.1
  123.6 43.4 %all_to_all.22.refs_1_ = bf16[32,4,896]{2,1,0:T(4,128)(2,1)S(1)} all-to-all(bf16[32,4,896]{2,1,0:T(4,128)(2,1)S(1)} %merge.1), channel_id=1, replica_groups={{16,17,18,19,20,21,22,23,24,25,26,27,28,29,30,31,0,1,2,3,4,5,6,7,8,9,10..., dimensions={0} | all-to-all | bytes 458752 | tf_op jit(solution)/shard_map/all_to_all | solution.py:170
  167.0 0.9 combine.1
  (1 shorter events, 0.0 us)
Async XLA Ops:
  2.2 56.0 %all-to-all-start = ((bf16[32,4,896]{2,1,0:T(4,128)(2,1)}), bf16[32,4,896]{2,1,0:T(4,128)(2,1)S(1)}, u32[]{:S(2)}, u32[]{:S(2)}) async-start(bf16[32,4,896]{2,1,0:T(4,128)(2,1)} %dispatch.1), calls=%async_computation | async-start | bytes 458752 | tf_op jit(solution)/shard_map/all_to_all | solution.py:170
  41.2 4.4 %copy-start = (s32[64,1]{0,1:T(1,128)S(1)}, s32[64,1]{0,1:T(1,128)}, u32[]{:S(2)}) copy-start(s32[64,1]{0,1:T(1,128)} %param.9) | copy-start | bytes 772
